TPU v7x, 128 devices: a whole 4x4x4 slice. The times are simulated.
128 devices in a mesh: section: 4 (over x), fsdp: 32 (over y, z, core).
Axes of the slice: x: 4, y: 4, z: 4, core: 2. Of those that a mesh axis runs over, the one named last changes fastest.
Arguments:
- inputs: bfloat16 [4096, 8192], P('fsdp'), may hold values from -6 to 6
- targets: bfloat16 [4096, 8192], P('fsdp'), may hold values from -6 to 6
- down_proj: bfloat16 [4, 8192, 128], P('section', 'fsdp'), may hold values from -0.0625 to 0.0625
- up_proj: bfloat16 [4, 8192, 128], P('section', 'fsdp'), may hold values from -0.5 to 0.5
- direction: float32 [4, 2, 8192, 128], P('section', None, 'fsdp'), may hold values from -6 to 6
- residual: float32 [4, 2, 8192, 128], P('section', None, 'fsdp'), may hold values from -6 to 6
Outputs:
- new_residual: float32 [4, 2, 8192, 128], P('section', None, 'fsdp')
- new_direction: float32 [4, 2, 8192, 128], P('section', None, 'fsdp')
All inputs are finite; a program needn't handle non-finite values.
Results may differ from a plain program's by a relative error of at most 0.027.
Values may be sent and summed in bfloat16 or wider, within the bound.
A program may use at most 128 MiB of HBM per device.

v0:
```python
import jax
import jax.numpy as jnp
from jax import lax
from jax.sharding import PartitionSpec as P

LENGTH = 128


norm_eps = 1e-05
damping = 1e-06


def shifted(value, axis, by):
    devices = lax.axis_size(axis)
    pairs = [(i, i + by) for i in range(devices) if 0 <= i + by < devices]
    return lax.ppermute(value, axis, pairs)


def silu_slope(values):
    sig = jax.nn.sigmoid(values)
    return sig * (1.0 + values * (1.0 - sig))


def contract_last(left, right):
    return lax.dot_general(
        left, right, (((1,), (1,)), ((), ())), preferred_element_type=jnp.float32
    )


def contract_first(left, right):
    return lax.dot_general(
        left, right, (((0,), (0,)), ((), ())), preferred_element_type=jnp.float32
    )


def store(buffer, value, slot, active):
    return jnp.where(active, lax.dynamic_update_index_in_dim(buffer, value, slot, 0), buffer)


def fetch(buffer, slot):
    return lax.dynamic_index_in_dim(buffer, slot, 0, keepdims=False)


def local(inputs, targets, down_proj, up_proj, direction, residual):
    sections = lax.axis_size("section")
    section_id = lax.axis_index("section")
    fsdp_count = lax.axis_size("fsdp")
    tok_rows, width = inputs.shape
    rank_width = down_proj.shape[2]
    own_rows = down_proj.shape[1]
    blocks = 1
    block_rows = tok_rows // blocks
    dir_bf = direction[0].astype(jnp.bfloat16)
    stacked = jnp.stack([down_proj[0], up_proj[0], dir_bf[0], dir_bf[1]])
    gathered = lax.all_gather(stacked, "fsdp", axis=1, tiled=True)
    w_down = gathered[0]
    w_up = gathered[1]
    tan_down = gathered[2]
    tan_up = gathered[3]
    input_blocks = inputs.reshape(blocks, block_rows, width)
    zero_rows = jnp.zeros((block_rows, width), jnp.bfloat16)
    recv_hidden = zero_rows
    recv_tangent = zero_rows
    saved_hidden = jnp.zeros((blocks, block_rows, width), jnp.bfloat16)
    saved_scale = jnp.ones((blocks, block_rows, 1), jnp.float32)
    saved_pre = jnp.zeros((blocks, block_rows, rank_width), jnp.float32)
    saved_act = jnp.zeros((blocks, block_rows, rank_width), jnp.bfloat16)
    out_hidden = jnp.zeros((blocks, block_rows, width), jnp.bfloat16)
    out_tangent = jnp.zeros((blocks, block_rows, width), jnp.bfloat16)
    is_first = section_id == 0
    is_last = section_id == sections - 1
    total_steps = sections + blocks - 1
    for step_now in range(total_steps):
        block_id = step_now - section_id
        active = (block_id >= 0) & (block_id < blocks)
        slot = jnp.clip(block_id, 0, blocks - 1)
        hidden_in = jnp.where(is_first, fetch(input_blocks, slot), recv_hidden)
        tangent_in = jnp.where(is_first, zero_rows, recv_tangent)
        hid = hidden_in.astype(jnp.float32)
        tan = tangent_in.astype(jnp.float32)
        scale_rms = jnp.sqrt(jnp.mean(hid * hid, axis=1, keepdims=True) + norm_eps)
        unit = hid / scale_rms
        normed = unit.astype(jnp.bfloat16)
        pre = jnp.dot(normed, w_down, preferred_element_type=jnp.float32)
        hidden_act = jax.nn.silu(pre).astype(jnp.bfloat16)
        normed_tan = (
            (tan - unit * jnp.mean(unit * tan, axis=1, keepdims=True)) / scale_rms
        ).astype(jnp.bfloat16)
        pre_tan = jnp.dot(normed_tan, w_down, preferred_element_type=jnp.float32) + jnp.dot(
            normed, tan_down, preferred_element_type=jnp.float32
        )
        act_tan = (silu_slope(pre) * pre_tan).astype(jnp.bfloat16)
        hidden_out = (hid + contract_last(hidden_act, w_up)).astype(jnp.bfloat16)
        tangent_out = (
            tan + contract_last(act_tan, w_up) + contract_last(hidden_act, tan_up)
        ).astype(jnp.bfloat16)
        saved_hidden = store(saved_hidden, hidden_in, slot, active)
        saved_scale = store(saved_scale, scale_rms, slot, active)
        saved_pre = store(saved_pre, pre, slot, active)
        saved_act = store(saved_act, hidden_act, slot, active)
        out_hidden = store(out_hidden, hidden_out, slot, active)
        out_tangent = store(out_tangent, tangent_out, slot, active)
        if step_now < total_steps - 1:
            recv_hidden, recv_tangent = shifted((hidden_out, tangent_out), "section", 1)
    error = out_hidden.reshape(tok_rows, width).astype(jnp.float32) - targets.astype(jnp.float32)
    per_token = jnp.sum(error * out_tangent.reshape(tok_rows, width).astype(jnp.float32), axis=1)
    seq_weight = jnp.sum(per_token.reshape(tok_rows // LENGTH, LENGTH), axis=1) / (LENGTH * width)
    cot_rows = (error * jnp.repeat(seq_weight, LENGTH)[:, None]).astype(jnp.bfloat16)
    cot_blocks = cot_rows.reshape(blocks, block_rows, width)
    recv_cot = zero_rows
    saved_cot = jnp.zeros((blocks, block_rows, width), jnp.bfloat16)
    saved_precot = jnp.zeros((blocks, block_rows, rank_width), jnp.bfloat16)
    for step_now in range(total_steps):
        block_id = step_now - (sections - 1 - section_id)
        active = (block_id >= 0) & (block_id < blocks)
        slot = jnp.clip(block_id, 0, blocks - 1)
        cot_in = jnp.where(is_last, fetch(cot_blocks, slot), recv_cot)
        scale_rms = fetch(saved_scale, slot)
        unit = fetch(saved_hidden, slot).astype(jnp.float32) / scale_rms
        act_cot = jnp.dot(cot_in, w_up, preferred_element_type=jnp.float32)
        pre_cot = (act_cot * silu_slope(fetch(saved_pre, slot))).astype(jnp.bfloat16)
        normed_cot = contract_last(pre_cot, w_down)
        cot_out = (
            cot_in.astype(jnp.float32)
            + (normed_cot - unit * jnp.mean(unit * normed_cot, axis=1, keepdims=True)) / scale_rms
        ).astype(jnp.bfloat16)
        saved_cot = store(saved_cot, cot_in, slot, active)
        saved_precot = store(saved_precot, pre_cot, slot, active)
        if step_now < total_steps - 1:
            recv_cot = shifted(cot_out, "section", -1)
    normed_all = (
        (saved_hidden.astype(jnp.float32) / saved_scale)
        .astype(jnp.bfloat16)
        .reshape(tok_rows, width)
    )
    precot_all = saved_precot.reshape(tok_rows, rank_width)
    cot_all = saved_cot.reshape(tok_rows, width)
    act_all = saved_act.reshape(tok_rows, rank_width)
    grad_rows = lax.psum_scatter(
        jnp.concatenate(
            [contract_first(normed_all, precot_all), contract_first(cot_all, act_all)], axis=1
        ).astype(jnp.bfloat16),
        "fsdp",
        scatter_dimension=0,
        tiled=True,
    ).astype(jnp.float32)
    seqs_total = tok_rows * fsdp_count // LENGTH
    fisher = jnp.transpose(grad_rows.reshape(own_rows, 2, rank_width), (1, 0, 2)) / (
        seqs_total * LENGTH * width
    )
    dir_now = direction[0]
    res_now = residual[0]
    product = fisher + damping * dir_now
    norm_old = lax.psum(jnp.sum(res_now * res_now), ("section", "fsdp"))
    alpha = norm_old / lax.psum(jnp.sum(dir_now * product), ("section", "fsdp"))
    new_res = res_now - alpha * product
    norm_new = lax.psum(jnp.sum(new_res * new_res), ("section", "fsdp"))
    new_dir = new_res + norm_new / norm_old * dir_now
    return (new_res[None], new_dir[None])


def solution(mesh):
    in_specs = (
        P("fsdp", None),
        P("fsdp", None),
        P("section", "fsdp", None),
        P("section", "fsdp", None),
        P("section", None, "fsdp", None),
        P("section", None, "fsdp", None),
    )
    out_specs = (P("section", None, "fsdp", None), P("section", None, "fsdp", None))
    return jax.shard_map(local, mesh=mesh, in_specs=in_specs, out_specs=out_specs, check_vma=False)
```

profile of v0, /device:TPU:1, one launch (start us, length us, event | category | flops | bytes accessed | tf_op | source)
XLA Modules:
  0.0 782.3 jit_solution(6427621794513764293)
XLA Ops:
  12.2 55.4 %all-gather.2.cloned.1.call-done = bf16[4,8192,128]{2,1,0:T(8,128)(2,1)} async-done(((bf16[4,256,128]{2,1,0:T(8,128)(2,1)}), bf16[4,8192,128]{2,1,0:T(8,128)(2,1)}) %all-gather.2.cloned.1.call-update) | async-done | bytes 8388624 | tf_op jit(solution)/shard_map/all_gather | solution.py:55
  75.7 44.6 %collective-permute-done = bf16[128,8192]{1,0:T(8,128)(2,1)S(1)} collective-permute-done((bf16[128,8192]{1,0:T(8,128)(2,1)S(1)}, bf16[128,8192]{1,0:T(8,128)(2,1)S(1)}, u32[]{:S(2)}, u32[]{:S(2)}) %collective-permute-start) | collective-permute-done | bytes 2097184 | tf_op jit(solution)/shard_map/ppermute | solution.py:16
  125.4 5.4 collective-permute-start.1
  132.0 5.6 fusion.95
  137.6 4.9 fusion.7
  146.1 4.4 fusion.53
  152.9 20.8 %collective-permute-done.1 = bf16[128,8192]{1,0:T(8,128)(2,1)} collective-permute-done((bf16[128,8192]{1,0:T(8,128)(2,1)}, bf16[128,8192]{1,0:T(8,128)(2,1)}, u32[]{:S(2)}, u32[]{:S(2)}) %collective-permute-start.1) | collective-permute-done | bytes 2097184 | tf_op jit(solution)/shard_map/ppermute | solution.py:16
  175.7 42.9 %collective-permute-done.3 = bf16[128,8192]{1,0:T(8,128)(2,1)} collective-permute-done((bf16[128,8192]{1,0:T(8,128)(2,1)}, bf16[128,8192]{1,0:T(8,128)(2,1)}, u32[]{:S(2)}, u32[]{:S(2)}) %collective-permute-start.3) | collective-permute-done | bytes 2097184 | tf_op jit(solution)/shard_map/ppermute | solution.py:16
  219.5 8.0 %fusion.8 = bf16[128,8192]{1,0:T(8,128)(2,1)} fusion(f32[128,8192]{1,0:T(8,128)} %fusion.53, bf16[128,8192]{1,0:T(8,128)(2,1)} %collective-permute-done.3, pred[]{:T(512)S(6)} %eq.6, f32[128,128]{1,0:T(8,128)S(1)} %fusion.49, f32[128]{0:T(128)S(1)} %broadcast_multiply_fusion.5, f32[128]{0:T(128)S(1)} %add_sqrt_fusion.2, f32[128,128]{1,0:T(8,128)S(1)} %fusion.107, ...), kind=kOutput, calls=%fused_computation.16 | convolution fusion | flops 550666240 | bytes 16910336 | tf_op jit(solution)/shard_map/dot_general | solution.py:25
  227.5 6.4 collective-permute-start.4
  237.1 3.7 fusion.5
  240.7 4.3 collective-permute-start.2
  245.0 4.3 fusion.52
  251.7 25.3 %collective-permute-done.4 = bf16[128,8192]{1,0:T(8,128)(2,1)S(1)} collective-permute-done((bf16[128,8192]{1,0:T(8,128)(2,1)}, bf16[128,8192]{1,0:T(8,128)(2,1)S(1)}, u32[]{:S(2)}, u32[]{:S(2)}) %collective-permute-start.4) | collective-permute-done | bytes 2097184 | tf_op jit(solution)/shard_map/ppermute | solution.py:16
  278.3 8.0 %fusion.9 = bf16[128,8192]{1,0:T(8,128)(2,1)} fusion(f32[128,8192]{1,0:T(8,128)} %fusion.52, bf16[128,8192]{1,0:T(8,128)(2,1)} %copy-done.15, pred[]{:T(512)S(6)} %eq.6, f32[128,128]{1,0:T(8,128)S(1)} %fusion.48, f32[128]{0:T(128)S(1)} %broadcast_multiply_fusion.4, f32[128]{0:T(128)S(1)} %add_sqrt_fusion.1, f32[128,128]{1,0:T(8,128)S(1)} %fusion.104, ...), kind=kOutput, calls=%fused_computation.17 | convolution fusion | flops 550666240 | bytes 16910336 | tf_op jit(solution)/shard_map/dot_general | solution.py:25
  286.3 4.9 collective-permute-start.5
  291.2 30.7 %collective-permute-done.2 = bf16[128,8192]{1,0:T(8,128)(2,1)} collective-permute-done((bf16[128,8192]{1,0:T(8,128)(2,1)}, bf16[128,8192]{1,0:T(8,128)(2,1)}, u32[]{:S(2)}, u32[]{:S(2)}) %collective-permute-start.2) | collective-permute-done | bytes 2097184 | tf_op jit(solution)/shard_map/ppermute | solution.py:16
  322.8 3.6 add_multiply_fusion
  331.7 4.0 fusion.13
  335.7 31.2 %collective-permute-done.5 = bf16[128,8192]{1,0:T(8,128)(2,1)S(1)} collective-permute-done((bf16[128,8192]{1,0:T(8,128)(2,1)}, bf16[128,8192]{1,0:T(8,128)(2,1)S(1)}, u32[]{:S(2)}, u32[]{:S(2)}) %collective-permute-start.5) | collective-permute-done | bytes 2097184 | tf_op jit(solution)/shard_map/ppermute | solution.py:16
  368.2 10.4 %fusion.97 = f32[]{:T(128)} fusion(f32[128,8192]{1,0:T(8,128)} %fusion.13, bf16[128,8192]{1,0:T(8,128)(2,1)} %fusion.9, bf16[128,8192]{1,0:T(8,128)(2,1)} %fusion.8, bf16[128,8192]{1,0:T(8,128)(2,1)} %fusion.7, pred[]{:T(512)S(6)} %and.28, pred[]{:T(512)S(6)} %and.27, pred[]{:T(512)S(6)} %and.26, f32[128,8192]{1,0:T(8,128)} %fusion.51, ...), kind=kOutput, calls=%fused_computation.123 | convolution fusion | flops 558006272 | bytes 25300996 | tf_op jit(solution)/shard_map/dot_general | solution.py:25
  386.0 5.6 multiply_reduce_fusion.2
  391.7 5.0 add_convert_fusion.2
  398.1 46.3 %collective-permute-done.6 = bf16[128,8192]{1,0:T(8,128)(2,1)S(1)} collective-permute-done((bf16[128,8192]{1,0:T(8,128)(2,1)S(1)}, bf16[128,8192]{1,0:T(8,128)(2,1)S(1)}, u32[]{:S(2)}, u32[]{:S(2)}) %collective-permute-start.6) | collective-permute-done | bytes 2097184 | tf_op jit(solution)/shard_map/ppermute | solution.py:16
  449.1 44.2 %collective-permute-done.7 = bf16[128,8192]{1,0:T(8,128)(2,1)S(1)} collective-permute-done((bf16[128,8192]{1,0:T(8,128)(2,1)S(1)}, bf16[128,8192]{1,0:T(8,128)(2,1)S(1)}, u32[]{:S(2)}, u32[]{:S(2)}) %collective-permute-start.7) | collective-permute-done | bytes 2097184 | tf_op jit(solution)/shard_map/ppermute | solution.py:16
  499.3 43.5 %collective-permute-done.8 = bf16[128,8192]{1,0:T(8,128)(2,1)} collective-permute-done((bf16[128,8192]{1,0:T(8,128)(2,1)}, bf16[128,8192]{1,0:T(8,128)(2,1)}, u32[]{:S(2)}, u32[]{:S(2)}) %collective-permute-start.8) | collective-permute-done | bytes 2097184 | tf_op jit(solution)/shard_map/ppermute | solution.py:16
  542.8 4.6 convolution_convert_fusion
  547.4 5.1 convolution_convert_fusion.1
  552.5 4.0 pad_maximum_fusion
  556.5 84.5 %reduce-scatter.2.cloned.1.call-done = bf16[256,256]{0,1:T(8,128)(2,1)} async-done(((bf16[8192,256]{0,1:T(8,128)(2,1)}), bf16[256,256]{0,1:T(8,128)(2,1)}) %reduce-scatter.2.cloned.1.call-update) | async-done | bytes 131088 | tf_op jit(solution)/shard_map/reduce_scatter | solution.py:139
  642.8 65.9 %all-reduce = (f32[]{:T(128)}, f32[]{:T(128)}) all-reduce(f32[]{:T(128)} %get-tuple-element.25, f32[]{:T(128)} %get-tuple-element.24), channel_id=1, replica_groups=mesh['section'=4,'fsdp'=32] {'section','fsdp'}, use_global_device_ids=true, to_apply=%region_1.2 | all-reduce | flops 2 | bytes 16 | tf_op jit(solution)/shard_map/psum | solution.py:154
  710.6 62.5 %psum.23 = f32[]{:T(128)} all-reduce(f32[]{:T(128)} %get-tuple-element.4), channel_id=1, replica_groups=mesh['section'=4,'fsdp'=32] {'section','fsdp'}, use_global_device_ids=true, to_apply=%region_18.19 | all-reduce | flops 1 | bytes 8 | tf_op jit(solution)/shard_map/psum | solution.py:157
  (106 shorter events, 64.3 us)
Async XLA Ops:
  7.2 60.5 %copy-start.3 = (bf16[128,8192]{1,0:T(8,128)(2,1)S(1)}, bf16[128,8192]{1,0:T(8,128)(2,1)}, u32[]{:S(2)}) copy-start(bf16[128,8192]{1,0:T(8,128)(2,1)} %param.6) | copy-start | bytes 6291460
  7.2 60.5 %all-gather.2.cloned.1.call-start = ((), (), s32[]{:S(2)}) async-start(), calls=%async_computation.1 | async-start | bytes 8650752 | tf_op jit(solution)/shard_map/all_gather | solution.py:55
  10.0 631.0 %reduce-scatter.2.cloned.1.call-start = ((), (), s32[]{:S(2)}) async-start(), calls=%async_computation.2 | async-start | bytes 4325376 | tf_op jit(solution)/shard_map/reduce_scatter | solution.py:139
  67.7 4.0 copy-start.2
  72.4 3.2 copy-start.19
  72.4 47.9 %collective-permute-start = (bf16[128,8192]{1,0:T(8,128)(2,1)S(1)}, bf16[128,8192]{1,0:T(8,128)(2,1)S(1)}, u32[]{:S(2)}, u32[]{:S(2)}) collective-permute-start(bf16[128,8192]{1,0:T(8,128)(2,1)S(1)} %fusion.3), channel_id=1, source_target_pairs={{0,32},{32,64},{64,96},{1,33},{33,65},{65,97},{2,34},{34,66},{66,9... | collective-permute-start | bytes 6291464 | tf_op jit(solution)/shard_map/ppermute | solution.py:16
  125.4 48.3 %collective-permute-start.1 = (bf16[128,8192]{1,0:T(8,128)(2,1)}, bf16[128,8192]{1,0:T(8,128)(2,1)}, u32[]{:S(2)}, u32[]{:S(2)}) collective-permute-start(bf16[128,8192]{1,0:T(8,128)(2,1)} %fusion.4), channel_id=1, source_target_pairs={{0,32},{32,64},{64,96},{1,33},{33,65},{65,97},{2,34},{34,66},{66,9... | collective-permute-start | bytes 6291464 | tf_op jit(solution)/shard_map/ppermute | solution.py:16
  142.5 76.0 %collective-permute-start.3 = (bf16[128,8192]{1,0:T(8,128)(2,1)}, bf16[128,8192]{1,0:T(8,128)(2,1)}, u32[]{:S(2)}, u32[]{:S(2)}) collective-permute-start(bf16[128,8192]{1,0:T(8,128)(2,1)} %fusion.7), channel_id=1, source_target_pairs={{0,32},{32,64},{64,96},{1,33},{33,65},{65,97},{2,34},{34,66},{66,9... | collective-permute-start | bytes 6291464 | tf_op jit(solution)/shard_map/ppermute | solution.py:16
  146.1 4.4 copy-start.5
  227.5 49.5 %collective-permute-start.4 = (bf16[128,8192]{1,0:T(8,128)(2,1)}, bf16[128,8192]{1,0:T(8,128)(2,1)S(1)}, u32[]{:S(2)}, u32[]{:S(2)}) collective-permute-start(bf16[128,8192]{1,0:T(8,128)(2,1)} %fusion.8), channel_id=1, source_target_pairs={{0,32},{32,64},{64,96},{1,33},{33,65},{65,97},{2,34},{34,66},{66,9... | collective-permute-start | bytes 6291464 | tf_op jit(solution)/shard_map/ppermute | solution.py:16
  233.9 3.1 copy-start.7
  240.7 81.2 %collective-permute-start.2 = (bf16[128,8192]{1,0:T(8,128)(2,1)}, bf16[128,8192]{1,0:T(8,128)(2,1)}, u32[]{:S(2)}, u32[]{:S(2)}) collective-permute-start(bf16[128,8192]{1,0:T(8,128)(2,1)} %fusion.5), channel_id=1, source_target_pairs={{0,32},{32,64},{64,96},{1,33},{33,65},{65,97},{2,34},{34,66},{66,9... | collective-permute-start | bytes 6291464 | tf_op jit(solution)/shard_map/ppermute | solution.py:16
  286.3 80.6 %collective-permute-start.5 = (bf16[128,8192]{1,0:T(8,128)(2,1)}, bf16[128,8192]{1,0:T(8,128)(2,1)S(1)}, u32[]{:S(2)}, u32[]{:S(2)}) collective-permute-start(bf16[128,8192]{1,0:T(8,128)(2,1)} %fusion.9), channel_id=1, source_target_pairs={{0,32},{32,64},{64,96},{1,33},{33,65},{65,97},{2,34},{34,66},{66,9... | collective-permute-start | bytes 6291464 | tf_op jit(solution)/shard_map/ppermute | solution.py:16
  321.9 4.4 slice-start
  322.8 44.1 %copy-start.10 = (bf16[128,8192]{1,0:T(8,128)(2,1)}, bf16[128,8192]{1,0:T(8,128)(2,1)S(1)}, u32[]{:S(2)}) copy-start(bf16[128,8192]{1,0:T(8,128)(2,1)S(1)} %get-tuple-element.9) | copy-start | bytes 6291460
  322.8 4.0 slice-start.1
  329.5 1.6 copy-start.18
  329.5 2.2 copy-start.20
  381.7 3.1 copy-start.12
  381.8 3.1 copy-start.6
  381.8 3.6 copy-start.8
  381.8 4.2 copy-start.11
  386.0 5.7 copy-start.1
  391.6 103.8 %copy-start = (f32[128,8192]{1,0:T(8,128)}, f32[128,8192]{1,0:T(8,128)S(1)}, u32[]{:S(2)}) copy-start(f32[128,8192]{1,0:T(8,128)S(1)} %get-tuple-element.7) | copy-start | bytes 12582916
  391.6 53.4 %slice-start.2 = ((s8[8388608]{0:T(1024)(128)(4,1)}), s8[4194304]{0:T(1024)(128)(4,1)S(1)}, s32[]{:S(2)}) async-start(s8[8388608]{0:T(1024)(128)(4,1)} %bitcast.101), calls=%async_computation.5 | async-start | bytes 8388608
  391.7 53.4 %slice-start.3 = ((s8[8388608]{0:T(1024)(128)(4,1)}), s8[4194304]{0:T(1024)(128)(4,1)S(1)}, s32[]{:S(2)}) async-start(s8[8388608]{0:T(1024)(128)(4,1)} %bitcast.101), calls=%async_computation.6 | async-start | bytes 8388608
  396.7 47.7 %collective-permute-start.6 = (bf16[128,8192]{1,0:T(8,128)(2,1)S(1)}, bf16[128,8192]{1,0:T(8,128)(2,1)S(1)}, u32[]{:S(2)}, u32[]{:S(2)}) collective-permute-start(bf16[128,8192]{1,0:T(8,128)(2,1)S(1)} %add_convert_fusion.2), channel_id=1, source_target_pairs={{32,0},{64,32},{96,64},{33,1},{65,33},{97,65},{34,2},{66,34},{98,6... | collective-permute-start | bytes 6291464 | tf_op jit(solution)/shard_map/ppermute | solution.py:16
  447.8 45.5 %collective-permute-start.7 = (bf16[128,8192]{1,0:T(8,128)(2,1)S(1)}, bf16[128,8192]{1,0:T(8,128)(2,1)S(1)}, u32[]{:S(2)}, u32[]{:S(2)}) collective-permute-start(bf16[128,8192]{1,0:T(8,128)(2,1)S(1)} %add_convert_fusion.1), channel_id=1, source_target_pairs={{32,0},{64,32},{96,64},{33,1},{65,33},{97,65},{34,2},{66,34},{98,6... | collective-permute-start | bytes 6291464 | tf_op jit(solution)/shard_map/ppermute | solution.py:16
  498.0 44.8 %collective-permute-start.8 = (bf16[128,8192]{1,0:T(8,128)(2,1)}, bf16[128,8192]{1,0:T(8,128)(2,1)}, u32[]{:S(2)}, u32[]{:S(2)}) collective-permute-start(bf16[128,8192]{1,0:T(8,128)(2,1)} %add_convert_fusion), channel_id=1, source_target_pairs={{32,0},{64,32},{96,64},{33,1},{65,33},{97,65},{34,2},{66,34},{98,6... | collective-permute-start | bytes 6291464 | tf_op jit(solution)/shard_map/ppermute | solution.py:16
  556.5 85.6 %copy-start.13 = (f32[1,2,256,128]{3,2,1,0:T(8,128)S(1)}, f32[1,2,256,128]{3,2,1,0:T(8,128)}, u32[]{:S(2)}) copy-start(f32[1,2,256,128]{3,2,1,0:T(8,128)} %param.10) | copy-start | bytes 786436
  556.5 85.6 %copy-start.16 = (f32[1,2,256,128]{3,2,1,0:T(8,128)S(1)}, f32[1,2,256,128]{3,2,1,0:T(8,128)}, u32[]{:S(2)}) copy-start(f32[1,2,256,128]{3,2,1,0:T(8,128)} %param.11) | copy-start | bytes 786436
  710.6 64.6 %copy-start.17 = (f32[2,256,128]{2,1,0:T(8,128)}, f32[2,256,128]{2,1,0:T(8,128)S(1)}, u32[]{:S(2)}) copy-start(f32[2,256,128]{2,1,0:T(8,128)S(1)} %get-tuple-element.5) | copy-start | bytes 786436
  (4 other events, 5.6 us)
Sparse Core Ops, SparseCore 0:
  10.9 56.6 all-gather.1
  556.6 84.3 reduce-scatter.1
where the time goes:
time: 790 us; the launch traced here: 782 us
  waiting for transfers between devices  470 us (59%)
  blocking collectives  128 us (16%)
  matrix products  96.7 us (12%)
  starting transfers between devices  31.9 us (4%)
  other arithmetic  31.8 us (4%)
  between operations  18.1 us (2%)
    ppermute x9, waiting for transfers between devices, shifted(): return lax.ppermute(value, axis, pairs)  330 us
    reduce_scatter x1, waiting for transfers between devices, local(): lax.psum_scatter(jnp.concatenate([contract_first(normed_all, precot_all),...  84.5 us
    psum x1, blocking collectives, local(): norm_old = lax.psum(jnp.sum(res_now * res_now), ('section', 'fsdp'))  65.9 us
    dot_general x15, matrix products, contract_last(): lax.dot_general(left, right, (((1,), (1,)), ((), ())), preferred_element_...  65.8 us
    psum x1, blocking collectives, local(): norm_new = lax.psum(jnp.sum(new_res * new_res), ('section', 'fsdp'))  62.5 us
    all_gather x1, waiting for transfers between devices, local(): gathered = lax.all_gather(stacked, 'fsdp', axis=1, tiled=True)  55.4 us
    ppermute x9, starting transfers between devices, shifted(): return lax.ppermute(value, axis, pairs)  31.8 us
  transfers between devices with their start and end apart: 11, of which 11 were waited for; matrix products, arithmetic and copies ran while one was open for 7% of the time, Pallas kernels for 0%

commit v1 on v0

v1 whole, which is shorter than its diff:
```python
import functools

import jax
import jax.numpy as jnp
from jax import lax
from jax.experimental import pallas as pl
from jax.experimental.pallas import tpu as pltpu
from jax.sharding import PartitionSpec as P

MESH = pl.DeviceIdType.MESH
bf16 = jnp.bfloat16
f32 = jnp.float32

norm_eps = 1e-05
damping = 1e-06
N_LAYER = 4
SIDE = 4
CHIPS = 16

CROSS = {}
for _j in range(N_LAYER):
    for _l in range(_j + 1, N_LAYER):
        CROSS[(_j, _l)] = len(CROSS)
SELF = {}
for _j in range(N_LAYER):
    for _l in range(_j, N_LAYER):
        SELF[(_j, _l)] = len(CROSS) + len(SELF)
N_GRAM = len(CROSS) + len(SELF)


def dot_nn(a, b):
    return lax.dot_general(a, b, (((1,), (0,)), ((), ())), preferred_element_type=f32)


def dot_nt(a, b):
    return lax.dot_general(a, b, (((1,), (1,)), ((), ())), preferred_element_type=f32)


def dot_tn(a, b):
    return lax.dot_general(a, b, (((0,), (0,)), ((), ())), preferred_element_type=f32)


class Counter:
    def __init__(self):
        self.n = 0

    def take(self):
        self.n += 1
        return self.n - 1


N_SEM = 185


def kernel(
    x_hbm, y_hbm, a_ref, b_ref, dir_ref, res_ref,
    newres_ref, newdir_ref,
    xin, yin, xg, yg, xs, ys, xt, yt, w, pbf,
    prod, prod_out, prod_in, prodx_out, prodx_in,
    gram, gram_out, gram_in, gramx_out, gramx_in, gfull,
    act, ht, g, half_in, full_in, acc2, half2_in, full2_in, fin,
    gx, stat_out, stat_in, stat2_out, stat2_in, dv_out, dv_in,
    send_sem, recv_sem, local_sem,
):
    tseq, width = xin.shape
    rank = a_ref.shape[1]
    own = a_ref.shape[0]
    pr = own // N_LAYER
    feats = CHIPS * pr
    tq = tseq // N_LAYER
    quad = SIDE * pr
    sx = lax.axis_index("section")
    f = lax.axis_index("fsdp")
    c = lax.rem(f, 2)
    z = lax.rem(lax.div(f, 2), SIDE)
    y = lax.div(f, 2 * SIDE)
    me_yz = y * SIDE + z

    def up(v, k):
        return lax.rem(v + k + SIDE, SIDE)

    def fs(yy, zz, cc):
        return (yy * SIDE + zz) * 2 + cc

    barrier = pltpu.get_barrier_semaphore()
    for k in range(1, 8):
        px = up(sx, k // 2)
        pc = lax.rem(c + k, 2)
        pl.semaphore_signal(barrier, inc=1, device_id=(px, fs(y, z, pc)), device_id_type=MESH)
    for k in range(1, CHIPS):
        pl.semaphore_signal(
            barrier, inc=1, device_id=(sx, fs(up(y, k // SIDE), up(z, k % SIDE), c)), device_id_type=MESH
        )

    load_x = pltpu.make_async_copy(x_hbm, xin, local_sem.at[0])
    load_y = pltpu.make_async_copy(y_hbm, yin, local_sem.at[1])
    load_x.start()
    load_y.start()
    pbf[...] = dir_ref[...].astype(bf16)

    pl.semaphore_wait(barrier, 7 + CHIPS - 1)

    counter = Counter()
    pending = []

    def send(src, dst, dev):
        k = counter.take()
        copy = pltpu.make_async_remote_copy(
            src_ref=src, dst_ref=dst, send_sem=send_sem.at[k], recv_sem=recv_sem.at[k],
            device_id=dev, device_id_type=MESH,
        )
        copy.start()
        pending.append(copy)
        return k

    def arrive(k, dst):
        pltpu.make_async_remote_copy(
            src_ref=dst, dst_ref=dst, send_sem=send_sem.at[k], recv_sem=recv_sem.at[k],
            device_id=(sx, f), device_id_type=MESH,
        ).wait_recv()

    sib = (sx, fs(y, z, 1 - c))

    def line(k):
        return (up(sx, k), f)

    def rows(ref, at, size):
        return ref.at[pl.ds(pl.multiple_of(at * size, size), size)]

    def cols(at):
        return pl.ds(pl.multiple_of(at * rank, rank), rank)

    def spread(srcs, arrs):
        keys = []
        for src, arr in zip(srcs, arrs):
            for k in range(1, N_LAYER):
                to = up(sx, k)
                keys.append((arr, k, send(rows(src, to, pr), w.at[arr, me_yz, :, cols(sx)], line(k))))
        copies = []
        for n, (src, arr) in enumerate(zip(srcs, arrs)):
            copy = pltpu.make_async_copy(
                rows(src, sx, pr), w.at[arr, me_yz, :, cols(sx)], local_sem.at[2 + arr]
            )
            copy.start()
            copies.append(copy)
        return keys, copies

    def spread_done(keys, copies):
        for copy in copies:
            copy.wait()
        for arr, k, key in keys:
            arrive(key, w.at[arr, me_yz, :, cols(up(sx, -k))])

    ab_keys = spread((a_ref, b_ref), (0, 1))
    p_keys = spread((pbf.at[0], pbf.at[1]), (2, 3))

    half = pr // 2
    lo, hi = pl.ds(0, half), pl.ds(half, half)

    class Gather:
        def __init__(self, arr, first):
            self.arr, self.first, self.key = arr, first, {}

        def blk(self, i, j):
            dy, dz = (i, j) if self.first == "y" else (j, i)
            return up(y, dy) * SIDE + up(z, dz)

        def dev(self, i, j):
            dy, dz = (i, j) if self.first == "y" else (j, i)
            return (sx, fs(up(y, dy), up(z, dz), c))

        def ref(self, i, j, part=None):
            r = w.at[self.arr, self.blk(i, j)]
            return r if part is None else w.at[self.arr, self.blk(i, j), part]

        def push(self, name, ref, di, dj):
            self.key[name] = send(ref, ref, self.dev(di, dj))

        def start(self):
            self.push("r", self.ref(0, 0), 1, 0)
            self.push("l", self.ref(0, 0), -1, 0)
            self.second(0)

        def second(self, i):
            self.push(("r", i), self.ref(i, 0), 0, 1)
            self.push(("l", i), self.ref(i, 0), 0, -1)

        def relay(self):
            arrive(self.key["r"], self.ref(-1, 0))
            self.push("rh", self.ref(-1, 0, lo), 1, 0)
            arrive(self.key["l"], self.ref(1, 0))
            self.push("lh", self.ref(1, 0, hi), -1, 0)
            self.second(-1)
            self.second(1)

        def relay_far(self):
            arrive(self.key["rh"], self.ref(2, 0, lo))
            arrive(self.key["lh"], self.ref(2, 0, hi))
            self.second(2)

        def relay_second(self, i):
            arrive(self.key[("r", i)], self.ref(i, -1))
            self.push(("rh", i), self.ref(i, -1, lo), 0, 1)
            arrive(self.key[("l", i)], self.ref(i, 1))
            self.push(("lh", i), self.ref(i, 1, hi), 0, -1)

        def finish(self, i):
            arrive(self.key[("rh", i)], self.ref(i, 2, lo))
            arrive(self.key[("lh", i)], self.ref(i, 2, hi))

    ga, gb = Gather(0, "y"), Gather(1, "z")
    gpa, gpb = Gather(2, "y"), Gather(3, "z")
    spread_done(*ab_keys)
    ga.start()
    gb.start()

    load_x.wait()
    load_y.wait()

    def pick(src, dst, cc, put):
        for p in range(0, CHIPS, 2):
            got = []
            for q in (p, p + 1):
                shard = src[:, pl.ds(pl.multiple_of((2 * q + cc) * own, own), own)]
                piece = shard[:, 0:pr]
                for k in range(1, N_LAYER):
                    piece = jnp.where(sx == k, shard[:, k * pr : (k + 1) * pr], piece)
                got.append(piece)
            put(dst, p, jnp.concatenate(got, axis=1))

    def put_other(dst, p, value):
        dst[:, p * pr : (p + 2) * pr] = value

    def put_own(dst, p, value):
        dst[pl.ds(pl.multiple_of(c * tseq, tseq), tseq), p * pr : (p + 2) * pr] = value

    pick(xin, xs, 1 - c, put_other)
    my_rows = pl.ds(pl.multiple_of(c * tseq, tseq), tseq)
    its_rows = pl.ds(pl.multiple_of((1 - c) * tseq, tseq), tseq)
    key_xs = send(xs, xg.at[my_rows], sib)
    pick(yin, ys, 1 - c, put_other)
    key_ys = send(ys, yg.at[my_rows], sib)
    pick(xin, xg, c, put_own)
    pick(yin, yg, c, put_own)

    ga.relay()
    gb.relay()
    ga.relay_second(0)
    gb.relay_second(0)

    xq = xin[pl.ds(pl.multiple_of(sx * tq, tq), tq), :].astype(f32)
    norm = jnp.sum(xq * xq, axis=1, keepdims=True)
    res = res_ref[...]
    direc = dir_ref[...]

    ga.relay_far()
    gb.relay_far()
    arrive(key_xs, xg.at[its_rows])
    arrive(key_ys, yg.at[its_rows])
    xt[...] = xg[...].astype(f32).T.astype(bf16)
    yt[...] = yg[...].astype(f32).T.astype(bf16)
    for i in (-1, 1, 2):
        ga.relay_second(i)
        gb.relay_second(i)
    spread_done(*p_keys)
    gpa.start()
    gpb.start()
    for i in (0, -1, 1, 2):
        ga.finish(i)
        gb.finish(i)

    wide = N_LAYER * rank
    wa = w[0].reshape(feats, wide)
    wb = w[1].reshape(feats, wide)
    xv = xg[...]
    yv = yg[...]
    prod[:, 0:wide] = dot_nn(xv, wa)
    prod[:, wide : 2 * wide] = dot_nn(xv, wb)
    prod[:, 2 * wide : 3 * wide] = dot_nn(yv, wb)
    prod_out[...] = prod[its_rows, :].astype(bf16)
    key_prod = send(prod_out, prod_in, sib)
    gpa.relay()
    gpb.relay()
    for j in range(N_LAYER):
        left = w[1, :, :, j * rank : (j + 1) * rank].reshape(feats, rank)
        if j < N_LAYER - 1:
            right = w[0, :, :, (j + 1) * rank : wide].reshape(feats, wide - (j + 1) * rank)
            block = dot_tn(left, right)
            for l in range(j + 1, N_LAYER):
                gram[CROSS[(j, l)]] = block[:, (l - j - 1) * rank : (l - j) * rank]
        right = w[1, :, :, j * rank : wide].reshape(feats, wide - j * rank)
        block = dot_tn(left, right)
        for l in range(j, N_LAYER):
            gram[SELF[(j, l)]] = block[:, (l - j) * rank : (l - j + 1) * rank]
    n_half = N_GRAM // 2
    my_gram = pl.ds(c * n_half, n_half)
    gram_out[...] = gram[pl.ds((1 - c) * n_half, n_half)].astype(bf16)
    key_gram = send(gram_out, gram_in, sib)
    gpa.relay_second(0)
    gpb.relay_second(0)

    arrive(key_prod, prod_in)
    pair = prod[my_rows, :] + prod_in[...].astype(f32)
    prod[my_rows, :] = pair
    prodx_out[...] = pair.astype(bf16)
    keys = []
    for k in range(1, N_LAYER):
        keys.append(send(rows(prodx_out, up(sx, k), tq), prodx_in.at[k - 1], line(k)))
    arrive(key_gram, gram_in)
    gpair = gram[my_gram] + gram_in[...].astype(f32)
    gram[my_gram] = gpair
    gramx_out[...] = gpair.astype(bf16)
    n_own = n_half // N_LAYER
    gkeys = []
    for k in range(1, N_LAYER):
        gkeys.append(send(gramx_out.at[pl.ds(up(sx, k) * n_own, n_own)], gramx_in.at[k - 1], line(k)))
    gpa.relay_far()
    gpb.relay_far()
    gsum = gram[pl.ds(c * n_half + sx * n_own, n_own)]
    for k in range(1, N_LAYER):
        arrive(gkeys[k - 1], gramx_in.at[k - 1])
        gsum = gsum + gramx_in[k - 1].astype(f32)
    mine = pl.ds(c * n_half + sx * n_own, n_own)
    gfull[mine] = gsum.astype(bf16)
    gkeys = []
    for k in range(1, N_LAYER):
        gkeys.append(send(gfull.at[mine], gfull.at[mine], line(k)))
    for i in (-1, 1):
        gpa.relay_second(i)
        gpb.relay_second(i)
    psum = prod[pl.ds(pl.multiple_of(c * tseq + sx * tq, tq), tq), :]
    for k in range(1, N_LAYER):
        arrive(keys[k - 1], prodx_in.at[k - 1])
        psum = psum + prodx_in[k - 1].astype(f32)
    for k in range(1, N_LAYER):
        arrive(gkeys[k - 1], gfull.at[pl.ds(c * n_half + up(sx, -k) * n_own, n_own)])
    key_gfull = send(gfull.at[my_gram], gfull.at[my_gram], sib)
    gpa.relay_second(2)
    gpb.relay_second(2)
    arrive(key_gfull, gfull.at[pl.ds((1 - c) * n_half, n_half)])

    def part(value, k):
        return value[:, k * rank : (k + 1) * rank]

    ha = [part(psum, l) for l in range(N_LAYER)]
    hb = [part(psum, N_LAYER + l) for l in range(N_LAYER)]
    yb = [part(psum, 2 * N_LAYER + l) for l in range(N_LAYER)]
    acts, slopes, rhos, pres, hbs = [], [], [], [], []
    for l in range(N_LAYER):
        rho = jnp.sqrt(norm / width + norm_eps)
        pre = ha[l] / rho
        sig = jax.nn.sigmoid(pre)
        a = (pre * sig).astype(bf16)
        hbs.append(hb[:l])
        before = hb[l]
        for m in range(l + 1, N_LAYER):
            ha[m] = ha[m] + dot_nn(a, gfull[CROSS[(l, m)]])
        nxt = []
        for m in range(N_LAYER):
            if l <= m:
                nxt.append(hb[m] + dot_nn(a, gfull[SELF[(l, m)]]))
            else:
                nxt.append(hb[m] + dot_nt(a, gfull[SELF[(m, l)]]))
        hb = nxt
        norm = norm + jnp.sum(a.astype(f32) * (before + hb[l]), axis=1, keepdims=True)
        acts.append(a)
        slopes.append(sig * (1.0 + pre * (1.0 - sig)))
        rhos.append(rho)
        pres.append(pre)
    cb = [hb[l] - yb[l] for l in range(N_LAYER)]
    qs = [None] * N_LAYER
    lane = lax.broadcasted_iota(jnp.int32, (tq, rank), 1)
    gains = jnp.zeros((tq, rank), f32)
    for l in range(N_LAYER - 1, -1, -1):
        cot = cb[l] * slopes[l]
        qs[l] = (cot / rhos[l]).astype(bf16)
        if l > 0:
            gain = jnp.sum(cot * pres[l], axis=1, keepdims=True) / (width * rhos[l] * rhos[l])
            gains = jnp.where(lane == l, gain, gains)
            for j in range(l):
                cb[j] = cb[j] + dot_nt(qs[l], gfull[CROSS[(j, l)]]) - gain * hbs[l][j]
    my_act = pl.ds(pl.multiple_of(c * tseq + sx * tq, tq), tq)
    for l in range(N_LAYER):
        act[my_act, l * rank : (l + 1) * rank] = acts[l]
        act[my_act, (N_LAYER + l) * rank : (N_LAYER + l + 1) * rank] = qs[l]
    act[my_act, 2 * N_LAYER * rank :] = gains.astype(bf16)
    keys = []
    for k in range(1, N_LAYER):
        keys.append(send(act.at[my_act], act.at[my_act], line(k)))
    for i in (0, -1, 1, 2):
        gpa.finish(i)
        gpb.finish(i)
    for k in range(1, N_LAYER):
        arrive(keys[k - 1], act.at[pl.ds(pl.multiple_of(c * tseq + up(sx, -k) * tq, tq), tq)])
    key_act = send(act.at[my_rows], act.at[my_rows], sib)
    arrive(key_act, act.at[its_rows])

    av = [act[:, l * rank : (l + 1) * rank] for l in range(N_LAYER)]
    qv = [act[:, (N_LAYER + l) * rank : (N_LAYER + l + 1) * rank] for l in range(N_LAYER)]
    gain_t = act[:, 2 * N_LAYER * rank :].astype(f32).T
    d0 = jnp.zeros((quad, rank), f32)
    d1 = jnp.zeros((quad, rank), f32)
    for q in range(SIDE):
        fr = slice(q * quad, (q + 1) * quad)

        def wq(arr, l):
            return w[arr, q * SIDE : (q + 1) * SIDE, :, l * rank : (l + 1) * rank].reshape(quad, rank)

        h = xt[fr, :].astype(f32)
        hs = []
        for l in range(N_LAYER):
            hb16 = h.astype(bf16)
            hs.append(hb16)
            ht[l, fr, :] = hb16
            h = hb16.astype(f32) + dot_nt(wq(1, l), av[l])
        cot = (h - yt[fr, :].astype(f32)).astype(bf16)
        for l in range(N_LAYER - 1, -1, -1):
            ht[N_LAYER + l, fr, :] = cot
            for arr, left, right in ((2, hs[l], qv[l]), (3, cot, av[l])):
                pw = wq(arr, l).astype(f32)
                d0 = d0 + dot_nn(left[:, :tseq], right[:tseq]) * pw
                d1 = d1 + dot_nn(left[:, tseq:], right[tseq:]) * pw
            if l > 0:
                cot = (
                    cot.astype(f32) + dot_nt(wq(0, l), qv[l]) - gain_t[l : l + 1, :] * hs[l].astype(f32)
                ).astype(bf16)
    def fold(v):
        return jnp.sum(v.reshape(quad // 8, 8, rank), axis=0)

    dv_out[...] = jnp.concatenate([fold(d0), fold(d1)], axis=0)
    keys = []
    for k in range(1, 8):
        keys.append(send(dv_out, dv_in.at[k - 1], (up(sx, k // 2), fs(y, z, lax.rem(c + k, 2)))))
    dv = dv_out[...]
    for k in range(1, 8):
        arrive(keys[k - 1], dv_in.at[k - 1])
        dv = dv + dv_in[k - 1]
    s0 = jnp.sum(dv[:8], keepdims=True) / (tseq * width)
    s1 = jnp.sum(dv[8:], keepdims=True) / (tseq * width)
    token = lax.broadcasted_iota(jnp.int32, (2 * tseq, 1), 0)
    scale = jnp.where(token < tseq, s0, s1)
    qd = [(qv[l].astype(f32) * scale).astype(bf16) for l in range(N_LAYER)]
    ad = [(av[l].astype(f32) * scale).astype(bf16) for l in range(N_LAYER)]

    for arr, base, right in ((0, 0, qd), (1, N_LAYER, ad)):
        for l in range(N_LAYER):
            for q in range(SIDE):
                value = dot_nn(ht[base + l, q * quad : (q + 1) * quad, :], right[l])
                g[arr, q * SIDE : (q + 1) * SIDE, :, l * rank : (l + 1) * rank] = value.astype(bf16).reshape(
                    SIDE, pr, rank
                )

    class Scatter:
        def __init__(self, arr, first):
            self.arr, self.first, self.key = arr, first, {}

        def blk(self, i, j):
            dy, dz = (j, i) if self.first == "y" else (i, j)
            return up(y, dy) * SIDE + up(z, dz)

        def dev(self, i, j):
            dy, dz = (j, i) if self.first == "y" else (i, j)
            return (sx, fs(up(y, dy), up(z, dz), c))

        def start(self, i):
            far = self.blk(i, 2)
            n = i % SIDE
            self.key[("rh", i)] = send(g.at[self.arr, far, lo], half_in.at[self.arr, n, 0], self.dev(0, 1))
            self.key[("lh", i)] = send(g.at[self.arr, far, hi], half_in.at[self.arr, n, 1], self.dev(0, -1))

        def middle(self, i):
            n = i % SIDE
            arrive(self.key[("rh", i)], half_in.at[self.arr, n, 0])
            b = self.blk(i, 1)
            g[self.arr, b, lo] = (g[self.arr, b, lo].astype(f32) + half_in[self.arr, n, 0].astype(f32)).astype(bf16)
            self.key[("r", i)] = send(g.at[self.arr, b], full_in.at[self.arr, n, 0], self.dev(0, 1))
            arrive(self.key[("lh", i)], half_in.at[self.arr, n, 1])
            b = self.blk(i, -1)
            g[self.arr, b, hi] = (g[self.arr, b, hi].astype(f32) + half_in[self.arr, n, 1].astype(f32)).astype(bf16)
            self.key[("l", i)] = send(g.at[self.arr, b], full_in.at[self.arr, n, 1], self.dev(0, -1))

        def end(self, i):
            n = i % SIDE
            arrive(self.key[("r", i)], full_in.at[self.arr, n, 0])
            arrive(self.key[("l", i)], full_in.at[self.arr, n, 1])
            value = (
                g[self.arr, self.blk(i, 0)].astype(f32)
                + full_in[self.arr, n, 0].astype(f32)
                + full_in[self.arr, n, 1].astype(f32)
            )
            acc2[self.arr, n] = value
            return value

        def start2(self):
            fin[self.arr, 1] = acc2[self.arr, 2].astype(bf16)
            self.key["rh"] = send(fin.at[self.arr, 1, lo], half2_in.at[self.arr, 0], self.dev(1, 0))
            self.key["lh"] = send(fin.at[self.arr, 1, hi], half2_in.at[self.arr, 1], self.dev(-1, 0))

        def middle2(self):
            arrive(self.key["rh"], half2_in.at[self.arr, 0])
            acc2[self.arr, 1, lo] = acc2[self.arr, 1, lo] + half2_in[self.arr, 0].astype(f32)
            fin[self.arr, 2] = acc2[self.arr, 1].astype(bf16)
            self.key["r"] = send(fin.at[self.arr, 2], full2_in.at[self.arr, 0], self.dev(1, 0))
            arrive(self.key["lh"], half2_in.at[self.arr, 1])
            acc2[self.arr, 3, hi] = acc2[self.arr, 3, hi] + half2_in[self.arr, 1].astype(f32)
            fin[self.arr, 3] = acc2[self.arr, 3].astype(bf16)
            self.key["l"] = send(fin.at[self.arr, 3], full2_in.at[self.arr, 1], self.dev(-1, 0))

        def end2(self):
            arrive(self.key["r"], full2_in.at[self.arr, 0])
            arrive(self.key["l"], full2_in.at[self.arr, 1])
            value = (
                acc2[self.arr, 0] + full2_in[self.arr, 0].astype(f32) + full2_in[self.arr, 1].astype(f32)
            )
            fin[self.arr, 0] = value.astype(bf16)
            self.back = []
            for k in range(1, N_LAYER):
                to = up(sx, k)
                self.back.append(send(fin.at[self.arr, 0, :, cols(to)], gx.at[self.arr, sx], line(k)))
            gx[self.arr, sx] = fin[self.arr, 0, :, cols(sx)]

        def done(self):
            for k in range(1, N_LAYER):
                arrive(self.back[k - 1], gx.at[self.arr, up(sx, -k)])

    sa, sb = Scatter(0, "z"), Scatter(1, "y")
    both = (sa, sb)
    order = (2, 1, -1, 0)
    for i in order:
        for s in both:
            s.start(i)
    for i in order:
        for s in both:
            s.middle(i)
    for s in both:
        s.end(2)
        s.start2()
    for i in (1, -1):
        for s in both:
            s.end(i)
    for s in both:
        s.middle2()
    for s in both:
        s.end(0)
    for s in both:
        s.end2()
    for s in both:
        s.done()

    tokens_total = tseq * 2 * CHIPS
    shrink = 1.0 / (damping * tokens_total * width)
    grad = gx[...].astype(f32).reshape(2, own, rank)
    big = grad * shrink + direc

    def fold2(v):
        return jnp.sum(v.reshape(2 * own // 8, 8, rank), axis=0)

    stat_out[...] = jnp.concatenate([fold2(res * res), fold2(direc * big), fold2(res * big), fold2(big * big)], axis=0)
    keys = []
    for k in range(1, 8):
        keys.append(send(stat_out, stat_in.at[k - 1], (up(sx, k // 2), fs(y, z, lax.rem(c + k, 2)))))
    total = stat_out[...]
    for k in range(1, 8):
        arrive(keys[k - 1], stat_in.at[k - 1])
        total = total + stat_in[k - 1]
    stat2_out[...] = total
    keys = []
    for k in range(1, CHIPS):
        keys.append(send(stat2_out, stat2_in.at[k - 1], (sx, fs(up(y, k // SIDE), up(z, k % SIDE), c))))
    for k in range(1, CHIPS):
        arrive(keys[k - 1], stat2_in.at[k - 1])
        total = total + stat2_in[k - 1]
    rr = jnp.sum(total[0:8], keepdims=True)
    pq = jnp.sum(total[8:16], keepdims=True) * damping
    rp = jnp.sum(total[16:24], keepdims=True)
    pp = jnp.sum(total[24:32], keepdims=True)
    step = rr / pq * damping
    norm_new = rr - 2.0 * (step * rp) + step * (step * pp)
    beta = norm_new / rr
    new_res = res - step * big
    newres_ref[...] = new_res
    newdir_ref[...] = new_res + beta * direc
    for copy in pending:
        copy.wait_send()


def step_kernel(inputs, targets, down_proj, up_proj, direction, residual):
    tseq, width = inputs.shape
    _, own, rank = down_proj.shape
    pr = own // N_LAYER
    feats = CHIPS * pr
    tq = tseq // N_LAYER
    wide = N_LAYER * rank
    n_half = N_GRAM // 2
    n_own = n_half // N_LAYER
    vm = pltpu.VMEM
    scratch = [
        vm((tseq, width), bf16), vm((tseq, width), bf16),
        vm((2 * tseq, feats), bf16), vm((2 * tseq, feats), bf16),
        vm((tseq, feats), bf16), vm((tseq, feats), bf16),
        vm((feats, 2 * tseq), bf16), vm((feats, 2 * tseq), bf16),
        vm((4, CHIPS, pr, wide), bf16), vm((2, own, rank), bf16),
        vm((2 * tseq, 3 * wide), f32), vm((tseq, 3 * wide), bf16), vm((tseq, 3 * wide), bf16),
        vm((tseq, 3 * wide), bf16), vm((N_LAYER - 1, tq, 3 * wide), bf16),
        vm((N_GRAM, rank, rank), f32), vm((n_half, rank, rank), bf16), vm((n_half, rank, rank), bf16),
        vm((n_half, rank, rank), bf16), vm((N_LAYER - 1, n_own, rank, rank), bf16), vm((N_GRAM, rank, rank), bf16),
        vm((2 * tseq, 2 * wide + rank), bf16), vm((2 * N_LAYER, feats, 2 * tseq), bf16),
        vm((2, CHIPS, pr, wide), bf16),
        vm((2, SIDE, 2, pr // 2, wide), bf16), vm((2, SIDE, 2, pr, wide), bf16),
        vm((2, SIDE, pr, wide), f32),
        vm((2, 2, pr // 2, wide), bf16), vm((2, 2, pr, wide), bf16), vm((2, SIDE, pr, wide), bf16),
        vm((2, N_LAYER, pr, rank), bf16),
        vm((32, rank), f32), vm((7, 32, rank), f32), vm((32, rank), f32), vm((CHIPS - 1, 32, rank), f32),
        vm((16, rank), f32), vm((7, 16, rank), f32),
        pltpu.SemaphoreType.DMA((N_SEM,)), pltpu.SemaphoreType.DMA((N_SEM,)), pltpu.SemaphoreType.DMA((6,)),
    ]
    spec = pl.BlockSpec(memory_space=pltpu.VMEM)
    hbm = pl.BlockSpec(memory_space=pl.ANY)
    out = jax.ShapeDtypeStruct((2, own, rank), f32)
    new_res, new_dir = pl.pallas_call(
        kernel,
        out_shape=(out, out),
        in_specs=[hbm, hbm, spec, spec, spec, spec],
        out_specs=(spec, spec),
        scratch_shapes=scratch,
        compiler_params=pltpu.CompilerParams(
            collective_id=0, has_side_effects=True, vmem_limit_bytes=52 * 1024 * 1024
        ),
        cost_estimate=pl.CostEstimate(flops=4_000_000_000, bytes_accessed=8_000_000, transcendentals=0),
    )(inputs, targets, down_proj[0], up_proj[0], direction[0], residual[0])
    return new_res[None], new_dir[None]


def solution(mesh):
    in_specs = (
        P("fsdp", None),
        P("fsdp", None),
        P("section", "fsdp", None),
        P("section", "fsdp", None),
        P("section", None, "fsdp", None),
        P("section", None, "fsdp", None),
    )
    out_specs = (P("section", None, "fsdp", None), P("section", None, "fsdp", None))
    return jax.shard_map(step_kernel, mesh=mesh, in_specs=in_specs, out_specs=out_specs, check_vma=False)
```

time: 790 us -> 109 us (0.14)
  waiting for transfers between devices: 470 us -> 0 us
  blocking collectives: 128 us -> 0 us
  Pallas kernels: 0 us -> 103 us
  matrix products: 96.7 us -> 0 us
  starting transfers between devices: 31.9 us -> 0 us
  other arithmetic: 31.8 us -> 0 us
  between operations: 18.1 us -> 0.65 us
    ppermute x9 -> x0, waiting for transfers between devices: 330 us -> none  [shifted(): return lax.ppermute(value, axis, pairs)]
    psum x2 -> x0, blocking collectives: 128 us -> none  [the longest x1 65.9 us: local(): norm_old = lax.psum(jnp.sum(res_now * res_now), ('section', 'fsdp'))]
    pallas_call x0 -> x1, Pallas kernels: none -> 103 us  [step_kernel(): pl.pallas_call(kernel, out_shape=(out, out), in_specs=[hbm, hbm, spec, sp...]
    dot_general x28 -> x0, matrix products: 96.7 us -> none  [the longest x15 65.8 us: contract_last(): lax.dot_general(left, right, (((1,), (1,)), ((), ())), preferred_element_...]
    reduce_scatter x1 -> x0, waiting for transfers between devices: 84.5 us -> none  [local(): lax.psum_scatter(jnp.concatenate([contract_first(normed_all, precot_all),...]
    all_gather x1 -> x0, waiting for transfers between devices: 55.4 us -> none  [local(): gathered = lax.all_gather(stacked, 'fsdp', axis=1, tiled=True)]
    ppermute x9 -> x0, starting transfers between devices: 31.8 us -> none  [shifted(): return lax.ppermute(value, axis, pairs)]
    convert_element_type x5 -> x0, other arithmetic: 12.3 us -> none  [the longest x3 8.74 us: local(): cot_out = (cot_in.astype(jnp.float32) + (normed_cot - unit * jnp.mean(uni...]
  transfers between devices with their start and end apart: 11 -> 0, of which waited for: 11 -> 0; matrix products, arithmetic and copies ran while one was open for 7% -> 0% of each run, Pallas kernels for 0% -> 0%
where the time goes in v1:
time: 109 us
  Pallas kernels  103 us (94%)
  local copies, waits for them, and re-layouts  4.98 us (5%)
    pallas_call x1, Pallas kernels, step_kernel(): pl.pallas_call(kernel, out_shape=(out, out), in_specs=[hbm, hbm, spec, sp...  103 us
    unnamed x10, local copies, waits for them, and re-layouts  4.98 us

profile of v1, /device:TPU:1, one launch (start us, length us, event | category | flops | bytes accessed | tf_op | source)
XLA Modules:
  0.0 109.1 jit_solution(1824137631677518358)
XLA Ops:
  0.6 0.0 copy-start
  0.6 0.9 copy-done
  1.6 0.0 copy-start.1
  1.6 0.9 copy-done.1
  2.5 0.0 copy-start.2
  2.5 0.8 copy-done.2
  3.4 0.0 copy-start.3
  3.4 0.8 copy-done.3
  4.2 103.5 %shard_map.77 = (f32[2,256,128]{2,1,0:T(8,128)S(1)}, f32[2,256,128]{2,1,0:T(8,128)S(1)}) custom-call(bf16[128,8192]{1,0:T(8,128)(2,1)} %x_hbm.1, bf16[128,8192]{1,0:T(8,128)(2,1)} %y_hbm.1, bf16[256,128]{1,0:T(8,128)(2,1)S(1)} %bitcast.10, bf16[256,128]{1,0:T(8,128)(2,1)S(1)} %bitcast.11, f32[2,256,128]{2,1,0:T(8,128)S(1)} %bitcast.8, f32[2,256,128]{2,1,0:T(8,128)S(1)} %bitcast.9), custom_call_target="tpu_custom_call" | custom-call | flops 4000000000 | bytes 8000000 | tf_op jit(solution)/shard_map/pallas_call | solution.py:620
  107.7 0.7 copy.10
  108.4 0.7 copy.11
Async XLA Ops:
  0.6 1.0 copy-start
  1.6 0.9 copy-start.1
  2.5 0.8 copy-start.2
  3.4 0.8 copy-start.3

commit v2 on v1

--- a/solution.py
+++ b/solution.py
@@ -49,16 +49,16 @@
         return self.n - 1
 
 
-N_SEM = 185
+N_SEM = 119
 
 
 def kernel(
-    x_hbm, y_hbm, a_ref, b_ref, dir_ref, res_ref,
+    x_hbm, y_hbm, a_ref, b_ref, dir_hbm, res_hbm,
     newres_ref, newdir_ref,
-    xin, yin, xg, yg, xs, ys, xt, yt, w, pbf,
+    xin, yin, dir_ref, res_ref, xg, yg, xs, ys, xt, yt, w, pbf,
     prod, prod_out, prod_in, prodx_out, prodx_in,
     gram, gram_out, gram_in, gramx_out, gramx_in, gfull,
-    act, ht, g, half_in, full_in, acc2, half2_in, full2_in, fin,
+    act, ht, g, pair_in, acc2, block_in, fin,
     gx, stat_out, stat_in, stat2_out, stat2_in, dv_out, dv_in,
     send_sem, recv_sem, local_sem,
 ):
@@ -74,7 +74,6 @@
     c = lax.rem(f, 2)
     z = lax.rem(lax.div(f, 2), SIDE)
     y = lax.div(f, 2 * SIDE)
-    me_yz = y * SIDE + z
 
     def up(v, k):
         return lax.rem(v + k + SIDE, SIDE)
@@ -87,18 +86,22 @@
         px = up(sx, k // 2)
         pc = lax.rem(c + k, 2)
         pl.semaphore_signal(barrier, inc=1, device_id=(px, fs(y, z, pc)), device_id_type=MESH)
-    for k in range(1, CHIPS):
-        pl.semaphore_signal(
-            barrier, inc=1, device_id=(sx, fs(up(y, k // SIDE), up(z, k % SIDE), c)), device_id_type=MESH
-        )
+    for k in range(1, SIDE):
+        pl.semaphore_signal(barrier, inc=1, device_id=(sx, fs(up(y, k), z, c)), device_id_type=MESH)
+        pl.semaphore_signal(barrier, inc=1, device_id=(sx, fs(y, up(z, k), c)), device_id_type=MESH)
 
     load_x = pltpu.make_async_copy(x_hbm, xin, local_sem.at[0])
     load_y = pltpu.make_async_copy(y_hbm, yin, local_sem.at[1])
+    load_d = pltpu.make_async_copy(dir_hbm, dir_ref, local_sem.at[6])
+    load_r = pltpu.make_async_copy(res_hbm, res_ref, local_sem.at[7])
+    load_d.start()
     load_x.start()
     load_y.start()
+    load_r.start()
+    load_d.wait()
     pbf[...] = dir_ref[...].astype(bf16)
 
-    pl.semaphore_wait(barrier, 7 + CHIPS - 1)
+    pl.semaphore_wait(barrier, 7 + 2 * (SIDE - 1))
 
     counter = Counter()
     pending = []
@@ -135,11 +138,11 @@
         for src, arr in zip(srcs, arrs):
             for k in range(1, N_LAYER):
                 to = up(sx, k)
-                keys.append((arr, k, send(rows(src, to, pr), w.at[arr, me_yz, :, cols(sx)], line(k))))
+                keys.append((arr, k, send(rows(src, to, pr), w.at[arr, y, z, :, cols(sx)], line(k))))
         copies = []
         for n, (src, arr) in enumerate(zip(srcs, arrs)):
             copy = pltpu.make_async_copy(
-                rows(src, sx, pr), w.at[arr, me_yz, :, cols(sx)], local_sem.at[2 + arr]
+                rows(src, sx, pr), w.at[arr, y, z, :, cols(sx)], local_sem.at[2 + arr]
             )
             copy.start()
             copies.append(copy)
@@ -149,64 +152,55 @@
         for copy in copies:
             copy.wait()
         for arr, k, key in keys:
-            arrive(key, w.at[arr, me_yz, :, cols(up(sx, -k))])
+            arrive(key, w.at[arr, y, z, :, cols(up(sx, -k))])
 
     ab_keys = spread((a_ref, b_ref), (0, 1))
     p_keys = spread((pbf.at[0], pbf.at[1]), (2, 3))
-
-    half = pr // 2
-    lo, hi = pl.ds(0, half), pl.ds(half, half)
 
     class Gather:
         def __init__(self, arr, first):
             self.arr, self.first, self.key = arr, first, {}
 
-        def blk(self, i, j):
-            dy, dz = (i, j) if self.first == "y" else (j, i)
-            return up(y, dy) * SIDE + up(z, dz)
-
         def dev(self, i, j):
             dy, dz = (i, j) if self.first == "y" else (j, i)
             return (sx, fs(up(y, dy), up(z, dz), c))
 
-        def ref(self, i, j, part=None):
-            r = w.at[self.arr, self.blk(i, j)]
-            return r if part is None else w.at[self.arr, self.blk(i, j), part]
+        def block(self, i):
+            if self.first == "y":
+                return w.at[self.arr, up(y, i), z]
+            return w.at[self.arr, y, up(z, i)]
+
+        def pair(self, p, j):
+            if self.first == "y":
+                return w.at[self.arr, pl.ds(2 * p, 2), up(z, j)]
+            return w.at[self.arr, up(y, j), pl.ds(2 * p, 2)]
 
         def push(self, name, ref, di, dj):
             self.key[name] = send(ref, ref, self.dev(di, dj))
 
         def start(self):
-            self.push("r", self.ref(0, 0), 1, 0)
-            self.push("l", self.ref(0, 0), -1, 0)
-            self.second(0)
-
-        def second(self, i):
-            self.push(("r", i), self.ref(i, 0), 0, 1)
-            self.push(("l", i), self.ref(i, 0), 0, -1)
+            for i in (2, 1, -1):
+                self.push(i, self.block(0), i, 0)
+
+        def second(self):
+            for i in (1, -1, 2):
+                arrive(self.key[i], self.block(-i))
+            self.push("r1", self.pair(0, 0), 0, 1)
+            self.push("l1", self.pair(1, 0), 0, -1)
+            self.push("r2", self.pair(1, 0), 0, 1)
+            self.push("l2", self.pair(0, 0), 0, -1)
 
         def relay(self):
-            arrive(self.key["r"], self.ref(-1, 0))
-            self.push("rh", self.ref(-1, 0, lo), 1, 0)
-            arrive(self.key["l"], self.ref(1, 0))
-            self.push("lh", self.ref(1, 0, hi), -1, 0)
-            self.second(-1)
-            self.second(1)
-
-        def relay_far(self):
-            arrive(self.key["rh"], self.ref(2, 0, lo))
-            arrive(self.key["lh"], self.ref(2, 0, hi))
-            self.second(2)
-
-        def relay_second(self, i):
-            arrive(self.key[("r", i)], self.ref(i, -1))
-            self.push(("rh", i), self.ref(i, -1, lo), 0, 1)
-            arrive(self.key[("l", i)], self.ref(i, 1))
-            self.push(("lh", i), self.ref(i, 1, hi), 0, -1)
-
-        def finish(self, i):
-            arrive(self.key[("rh", i)], self.ref(i, 2, lo))
-            arrive(self.key[("lh", i)], self.ref(i, 2, hi))
+            arrive(self.key["r1"], self.pair(0, -1))
+            self.push("rr", self.pair(0, -1), 0, 1)
+            arrive(self.key["l1"], self.pair(1, 1))
+            self.push("ll", self.pair(1, 1), 0, -1)
+
+        def finish(self):
+            arrive(self.key["r2"], self.pair(1, -1))
+            arrive(self.key["l2"], self.pair(0, 1))
+            arrive(self.key["rr"], self.pair(0, 2))
+            arrive(self.key["ll"], self.pair(1, 2))
 
     ga, gb = Gather(0, "y"), Gather(1, "z")
     gpa, gpb = Gather(2, "y"), Gather(3, "z")
@@ -243,31 +237,28 @@
     pick(xin, xg, c, put_own)
     pick(yin, yg, c, put_own)
 
-    ga.relay()
-    gb.relay()
-    ga.relay_second(0)
-    gb.relay_second(0)
+    ga.second()
+    gb.second()
 
     xq = xin[pl.ds(pl.multiple_of(sx * tq, tq), tq), :].astype(f32)
     norm = jnp.sum(xq * xq, axis=1, keepdims=True)
+    load_r.wait()
     res = res_ref[...]
     direc = dir_ref[...]
 
-    ga.relay_far()
-    gb.relay_far()
+    spread_done(*p_keys)
+    gpa.start()
+    gpb.start()
     arrive(key_xs, xg.at[its_rows])
     arrive(key_ys, yg.at[its_rows])
     xt[...] = xg[...].astype(f32).T.astype(bf16)
     yt[...] = yg[...].astype(f32).T.astype(bf16)
-    for i in (-1, 1, 2):
-        ga.relay_second(i)
-        gb.relay_second(i)
-    spread_done(*p_keys)
-    gpa.start()
-    gpb.start()
-    for i in (0, -1, 1, 2):
-        ga.finish(i)
-        gb.finish(i)
+    ga.relay()
+    gb.relay()
+    gpa.second()
+    gpb.second()
+    ga.finish()
+    gb.finish()
 
     wide = N_LAYER * rank
     wa = w[0].reshape(feats, wide)
@@ -279,16 +270,14 @@
     prod[:, 2 * wide : 3 * wide] = dot_nn(yv, wb)
     prod_out[...] = prod[its_rows, :].astype(bf16)
     key_prod = send(prod_out, prod_in, sib)
-    gpa.relay()
-    gpb.relay()
     for j in range(N_LAYER):
-        left = w[1, :, :, j * rank : (j + 1) * rank].reshape(feats, rank)
+        left = w[1, :, :, :, j * rank : (j + 1) * rank].reshape(feats, rank)
         if j < N_LAYER - 1:
-            right = w[0, :, :, (j + 1) * rank : wide].reshape(feats, wide - (j + 1) * rank)
+            right = w[0, :, :, :, (j + 1) * rank : wide].reshape(feats, wide - (j + 1) * rank)
             block = dot_tn(left, right)
             for l in range(j + 1, N_LAYER):
                 gram[CROSS[(j, l)]] = block[:, (l - j - 1) * rank : (l - j) * rank]
-        right = w[1, :, :, j * rank : wide].reshape(feats, wide - j * rank)
+        right = w[1, :, :, :, j * rank : wide].reshape(feats, wide - j * rank)
         block = dot_tn(left, right)
         for l in range(j, N_LAYER):
             gram[SELF[(j, l)]] = block[:, (l - j) * rank : (l - j + 1) * rank]
@@ -296,8 +285,6 @@
     my_gram = pl.ds(c * n_half, n_half)
     gram_out[...] = gram[pl.ds((1 - c) * n_half, n_half)].astype(bf16)
     key_gram = send(gram_out, gram_in, sib)
-    gpa.relay_second(0)
-    gpb.relay_second(0)
 
     arrive(key_prod, prod_in)
     pair = prod[my_rows, :] + prod_in[...].astype(f32)
@@ -314,8 +301,8 @@
     gkeys = []
     for k in range(1, N_LAYER):
         gkeys.append(send(gramx_out.at[pl.ds(up(sx, k) * n_own, n_own)], gramx_in.at[k - 1], line(k)))
-    gpa.relay_far()
-    gpb.relay_far()
+    gpa.relay()
+    gpb.relay()
     gsum = gram[pl.ds(c * n_half + sx * n_own, n_own)]
     for k in range(1, N_LAYER):
         arrive(gkeys[k - 1], gramx_in.at[k - 1])
@@ -325,9 +312,6 @@
     gkeys = []
     for k in range(1, N_LAYER):
         gkeys.append(send(gfull.at[mine], gfull.at[mine], line(k)))
-    for i in (-1, 1):
-        gpa.relay_second(i)
-        gpb.relay_second(i)
     psum = prod[pl.ds(pl.multiple_of(c * tseq + sx * tq, tq), tq), :]
     for k in range(1, N_LAYER):
         arrive(keys[k - 1], prodx_in.at[k - 1])
@@ -335,8 +319,6 @@
     for k in range(1, N_LAYER):
         arrive(gkeys[k - 1], gfull.at[pl.ds(c * n_half + up(sx, -k) * n_own, n_own)])
     key_gfull = send(gfull.at[my_gram], gfull.at[my_gram], sib)
-    gpa.relay_second(2)
-    gpb.relay_second(2)
     arrive(key_gfull, gfull.at[pl.ds((1 - c) * n_half, n_half)])
 
     def part(value, k):
@@ -387,9 +369,8 @@
     keys = []
     for k in range(1, N_LAYER):
         keys.append(send(act.at[my_act], act.at[my_act], line(k)))
-    for i in (0, -1, 1, 2):
-        gpa.finish(i)
-        gpb.finish(i)
+    gpa.finish()
+    gpb.finish()
     for k in range(1, N_LAYER):
         arrive(keys[k - 1], act.at[pl.ds(pl.multiple_of(c * tseq + up(sx, -k) * tq, tq), tq)])
     key_act = send(act.at[my_rows], act.at[my_rows], sib)
@@ -404,7 +385,7 @@
         fr = slice(q * quad, (q + 1) * quad)
 
         def wq(arr, l):
-            return w[arr, q * SIDE : (q + 1) * SIDE, :, l * rank : (l + 1) * rank].reshape(quad, rank)
+            return w[arr, q, :, :, l * rank : (l + 1) * rank].reshape(quad, rank)
 
         h = xt[fr, :].astype(f32)
         hs = []
@@ -446,102 +427,75 @@
         for l in range(N_LAYER):
             for q in range(SIDE):
                 value = dot_nn(ht[base + l, q * quad : (q + 1) * quad, :], right[l])
-                g[arr, q * SIDE : (q + 1) * SIDE, :, l * rank : (l + 1) * rank] = value.astype(bf16).reshape(
-                    SIDE, pr, rank
+                g[arr, q, :, :, l * rank : (l + 1) * rank] = value.astype(bf16).reshape(SIDE, pr, rank)
+
+    class Scatter:
+        def __init__(self, arr, last):
+            self.arr, self.last, self.key = arr, last, {}
+            self.at = y if last == "y" else z
+
+        def dev(self, i, j):
+            dy, dz = (i, j) if self.last == "y" else (j, i)
+            return (sx, fs(up(y, dy), up(z, dz), c))
+
+        def pair(self, p, j):
+            if self.last == "y":
+                return self.arr, pl.ds(2 * p, 2), up(z, j)
+            return self.arr, up(y, j), pl.ds(2 * p, 2)
+
+        def push(self, n, p, j, dj):
+            self.key[n] = send(g.at[self.pair(p, j)], pair_in.at[self.arr, n], self.dev(0, dj))
+
+        def arrived(self, n):
+            arrive(self.key[n], pair_in.at[self.arr, n])
+            return pair_in[self.arr, n].astype(f32)
+
+        def start(self):
+            self.push(0, 0, 2, 1)
+            self.push(1, 1, 2, -1)
+            self.push(2, 1, 1, 1)
+            self.push(3, 0, -1, -1)
+
+        def middle(self):
+            at = self.pair(0, 1)
+            g[at] = (g[at].astype(f32) + self.arrived(0)).astype(bf16)
+            self.push(4, 0, 1, 1)
+            at = self.pair(1, -1)
+            g[at] = (g[at].astype(f32) + self.arrived(1)).astype(bf16)
+            self.push(5, 1, -1, -1)
+
+        def end(self):
+            acc2[self.arr, 2:4] = g[self.pair(1, 0)].astype(f32) + self.arrived(2) + self.arrived(5)
+            acc2[self.arr, 0:2] = g[self.pair(0, 0)].astype(f32) + self.arrived(3) + self.arrived(4)
+            fin[self.arr, 0:SIDE] = acc2[self.arr].astype(bf16)
+            for i in (2, 1, -1):
+                self.key[("s", i)] = send(
+                    fin.at[self.arr, up(self.at, i)], block_in.at[self.arr, i % SIDE - 1], self.dev(i, 0)
                 )
 
-    class Scatter:
-        def __init__(self, arr, first):
-            self.arr, self.first, self.key = arr, first, {}
-
-        def blk(self, i, j):
-            dy, dz = (j, i) if self.first == "y" else (i, j)
-            return up(y, dy) * SIDE + up(z, dz)
-
-        def dev(self, i, j):
-            dy, dz = (j, i) if self.first == "y" else (i, j)
-            return (sx, fs(up(y, dy), up(z, dz), c))
-
-        def start(self, i):
-            far = self.blk(i, 2)
-            n = i % SIDE
-            self.key[("rh", i)] = send(g.at[self.arr, far, lo], half_in.at[self.arr, n, 0], self.dev(0, 1))
-            self.key[("lh", i)] = send(g.at[self.arr, far, hi], half_in.at[self.arr, n, 1], self.dev(0, -1))
-
-        def middle(self, i):
-            n = i % SIDE
-            arrive(self.key[("rh", i)], half_in.at[self.arr, n, 0])
-            b = self.blk(i, 1)
-            g[self.arr, b, lo] = (g[self.arr, b, lo].astype(f32) + half_in[self.arr, n, 0].astype(f32)).astype(bf16)
-            self.key[("r", i)] = send(g.at[self.arr, b], full_in.at[self.arr, n, 0], self.dev(0, 1))
-            arrive(self.key[("lh", i)], half_in.at[self.arr, n, 1])
-            b = self.blk(i, -1)
-            g[self.arr, b, hi] = (g[self.arr, b, hi].astype(f32) + half_in[self.arr, n, 1].astype(f32)).astype(bf16)
-            self.key[("l", i)] = send(g.at[self.arr, b], full_in.at[self.arr, n, 1], self.dev(0, -1))
-
-        def end(self, i):
-            n = i % SIDE
-            arrive(self.key[("r", i)], full_in.at[self.arr, n, 0])
-            arrive(self.key[("l", i)], full_in.at[self.arr, n, 1])
-            value = (
-                g[self.arr, self.blk(i, 0)].astype(f32)
-                + full_in[self.arr, n, 0].astype(f32)
-                + full_in[self.arr, n, 1].astype(f32)
-            )
-            acc2[self.arr, n] = value
-            return value
-
-        def start2(self):
-            fin[self.arr, 1] = acc2[self.arr, 2].astype(bf16)
-            self.key["rh"] = send(fin.at[self.arr, 1, lo], half2_in.at[self.arr, 0], self.dev(1, 0))
-            self.key["lh"] = send(fin.at[self.arr, 1, hi], half2_in.at[self.arr, 1], self.dev(-1, 0))
-
-        def middle2(self):
-            arrive(self.key["rh"], half2_in.at[self.arr, 0])
-            acc2[self.arr, 1, lo] = acc2[self.arr, 1, lo] + half2_in[self.arr, 0].astype(f32)
-            fin[self.arr, 2] = acc2[self.arr, 1].astype(bf16)
-            self.key["r"] = send(fin.at[self.arr, 2], full2_in.at[self.arr, 0], self.dev(1, 0))
-            arrive(self.key["lh"], half2_in.at[self.arr, 1])
-            acc2[self.arr, 3, hi] = acc2[self.arr, 3, hi] + half2_in[self.arr, 1].astype(f32)
-            fin[self.arr, 3] = acc2[self.arr, 3].astype(bf16)
-            self.key["l"] = send(fin.at[self.arr, 3], full2_in.at[self.arr, 1], self.dev(-1, 0))
-
         def end2(self):
-            arrive(self.key["r"], full2_in.at[self.arr, 0])
-            arrive(self.key["l"], full2_in.at[self.arr, 1])
-            value = (
-                acc2[self.arr, 0] + full2_in[self.arr, 0].astype(f32) + full2_in[self.arr, 1].astype(f32)
-            )
-            fin[self.arr, 0] = value.astype(bf16)
+            value = acc2[self.arr, self.at]
+            for i in (1, -1, 2):
+                arrive(self.key[("s", i)], block_in.at[self.arr, i % SIDE - 1])
+                value = value + block_in[self.arr, i % SIDE - 1].astype(f32)
+            fin[self.arr, SIDE] = value.astype(bf16)
             self.back = []
             for k in range(1, N_LAYER):
                 to = up(sx, k)
-                self.back.append(send(fin.at[self.arr, 0, :, cols(to)], gx.at[self.arr, sx], line(k)))
-            gx[self.arr, sx] = fin[self.arr, 0, :, cols(sx)]
+                self.back.append(send(fin.at[self.arr, SIDE, :, cols(to)], gx.at[self.arr, sx], line(k)))
+            gx[self.arr, sx] = fin[self.arr, SIDE, :, cols(sx)]
 
         def done(self):
             for k in range(1, N_LAYER):
                 arrive(self.back[k - 1], gx.at[self.arr, up(sx, -k)])
 
-    sa, sb = Scatter(0, "z"), Scatter(1, "y")
-    both = (sa, sb)
-    order = (2, 1, -1, 0)
-    for i in order:
-        for s in both:
-            s.start(i)
-    for i in order:
-        for s in both:
-            s.middle(i)
+    both = (Scatter(0, "y"), Scatter(1, "z"))
     for s in both:
-        s.end(2)
-        s.start2()
-    for i in (1, -1):
-        for s in both:
-            s.end(i)
+        s.start()
     for s in both:
-        s.middle2()
+        s.middle()
     for s in both:
-        s.end(0)
+        s.end()
     for s in both:
         s.end2()
     for s in both:
@@ -596,23 +550,24 @@
     vm = pltpu.VMEM
     scratch = [
         vm((tseq, width), bf16), vm((tseq, width), bf16),
+        vm((2, own, rank), f32), vm((2, own, rank), f32),
         vm((2 * tseq, feats), bf16), vm((2 * tseq, feats), bf16),
         vm((tseq, feats), bf16), vm((tseq, feats), bf16),
         vm((feats, 2 * tseq), bf16), vm((feats, 2 * tseq), bf16),
-        vm((4, CHIPS, pr, wide), bf16), vm((2, own, rank), bf16),
+        vm((4, SIDE, SIDE, pr, wide), bf16), vm((2, own, rank), bf16),
         vm((2 * tseq, 3 * wide), f32), vm((tseq, 3 * wide), bf16), vm((tseq, 3 * wide), bf16),
         vm((tseq, 3 * wide), bf16), vm((N_LAYER - 1, tq, 3 * wide), bf16),
         vm((N_GRAM, rank, rank), f32), vm((n_half, rank, rank), bf16), vm((n_half, rank, rank), bf16),
         vm((n_half, rank, rank), bf16), vm((N_LAYER - 1, n_own, rank, rank), bf16), vm((N_GRAM, rank, rank), bf16),
         vm((2 * tseq, 2 * wide + rank), bf16), vm((2 * N_LAYER, feats, 2 * tseq), bf16),
-        vm((2, CHIPS, pr, wide), bf16),
-        vm((2, SIDE, 2, pr // 2, wide), bf16), vm((2, SIDE, 2, pr, wide), bf16),
+        vm((2, SIDE, SIDE, pr, wide), bf16),
+        vm((2, 6, 2, pr, wide), bf16),
         vm((2, SIDE, pr, wide), f32),
-        vm((2, 2, pr // 2, wide), bf16), vm((2, 2, pr, wide), bf16), vm((2, SIDE, pr, wide), bf16),
+        vm((2, 3, pr, wide), bf16), vm((2, SIDE + 1, pr, wide), bf16),
         vm((2, N_LAYER, pr, rank), bf16),
         vm((32, rank), f32), vm((7, 32, rank), f32), vm((32, rank), f32), vm((CHIPS - 1, 32, rank), f32),
         vm((16, rank), f32), vm((7, 16, rank), f32),
-        pltpu.SemaphoreType.DMA((N_SEM,)), pltpu.SemaphoreType.DMA((N_SEM,)), pltpu.SemaphoreType.DMA((6,)),
+        pltpu.SemaphoreType.DMA((N_SEM,)), pltpu.SemaphoreType.DMA((N_SEM,)), pltpu.SemaphoreType.DMA((8,)),
     ]
     spec = pl.BlockSpec(memory_space=pltpu.VMEM)
     hbm = pl.BlockSpec(memory_space=pl.ANY)
@@ -620,11 +575,11 @@
     new_res, new_dir = pl.pallas_call(
         kernel,
         out_shape=(out, out),
-        in_specs=[hbm, hbm, spec, spec, spec, spec],
+        in_specs=[hbm] * 6,
         out_specs=(spec, spec),
         scratch_shapes=scratch,
         compiler_params=pltpu.CompilerParams(
-            collective_id=0, has_side_effects=True, vmem_limit_bytes=52 * 1024 * 1024
+            collective_id=0, has_side_effects=True, vmem_limit_bytes=60 * 1024 * 1024
         ),
         cost_estimate=pl.CostEstimate(flops=4_000_000_000, bytes_accessed=8_000_000, transcendentals=0),
     )(inputs, targets, down_proj[0], up_proj[0], direction[0], residual[0])

time: 109 us -> 107 us (0.982)
  local copies, waits for them, and re-layouts: 4.98 us -> 3.34 us
    unnamed x10 -> x2, local copies, waits for them, and re-layouts: 4.98 us -> 3.34 us
where the time goes in v2:
time: 107 us
  Pallas kernels  103 us (96%)
  local copies, waits for them, and re-layouts  3.34 us (3%)
    pallas_call x1, Pallas kernels, step_kernel(): pl.pallas_call(kernel, out_shape=(out, out), in_specs=[hbm] * 6, out_spec...  103 us
    unnamed x2, local copies, waits for them, and re-layouts  3.34 us

profile of v2, /device:TPU:1, one launch (start us, length us, event | category | flops | bytes accessed | tf_op | source)
XLA Modules:
  0.0 107.1 jit_solution(4248689302599057008)
XLA Ops:
  0.6 103.1 %shard_map.77 = (f32[2,256,128]{2,1,0:T(8,128)}, f32[2,256,128]{2,1,0:T(8,128)}) custom-call(bf16[128,8192]{1,0:T(8,128)(2,1)} %x_hbm.1, bf16[128,8192]{1,0:T(8,128)(2,1)} %y_hbm.1, bf16[256,128]{1,0:T(8,128)(2,1)} %bitcast.10, bf16[256,128]{1,0:T(8,128)(2,1)} %bitcast.11, f32[2,256,128]{2,1,0:T(8,128)} %bitcast.8, f32[2,256,128]{2,1,0:T(8,128)} %bitcast.9), custom_call_target="tpu_custom_call" | custom-call | flops 4000000000 | bytes 8000000 | tf_op jit(solution)/shard_map/pallas_call | solution.py:575
  103.8 1.7 %copy.10 = f32[1,2,256,128]{3,2,1,0:T(8,128)} copy(f32[1,2,256,128]{3,2,1,0:T(8,128)} %bitcast.7) | data formatting | bytes 524288
  105.4 1.7 %copy.11 = f32[1,2,256,128]{3,2,1,0:T(8,128)} copy(f32[1,2,256,128]{3,2,1,0:T(8,128)} %bitcast.6) | data formatting | bytes 524288

commit v3 on v2

--- a/solution.py
+++ b/solution.py
@@ -49,7 +49,7 @@
         return self.n - 1
 
 
-N_SEM = 119
+N_SEM = 125
 
 
 def kernel(
@@ -155,7 +155,6 @@
             arrive(key, w.at[arr, y, z, :, cols(up(sx, -k))])
 
     ab_keys = spread((a_ref, b_ref), (0, 1))
-    p_keys = spread((pbf.at[0], pbf.at[1]), (2, 3))
 
     class Gather:
         def __init__(self, arr, first):
@@ -181,6 +180,21 @@
         def start(self):
             for i in (2, 1, -1):
                 self.push(i, self.block(0), i, 0)
+
+        def second_direct(self):
+            for i in (1, -1, 2):
+                arrive(self.key[i], self.block(-i))
+            for j in (2, 1, -1):
+                self.key[("d", j)] = send(self.whole(0), self.whole(0), self.dev(0, j))
+
+        def finish_direct(self):
+            for j in (1, -1, 2):
+                arrive(self.key[("d", j)], self.whole(-j))
+
+        def whole(self, j):
+            if self.first == "y":
+                return w.at[self.arr, :, up(z, j)]
+            return w.at[self.arr, up(y, j)]
 
         def second(self):
             for i in (1, -1, 2):
@@ -204,72 +218,66 @@
 
     ga, gb = Gather(0, "y"), Gather(1, "z")
     gpa, gpb = Gather(2, "y"), Gather(3, "z")
+    def pick(src, dst, cc, put):
+        odd = lax.rem(sx, 2) == 1
+        for p in range(0, CHIPS, 2):
+            tiles = []
+            for q in (p, p + 1):
+                at = (2 * q + cc) * own + lax.div(sx, 2) * (2 * pr)
+                tiles.append(src[:, pl.ds(pl.multiple_of(at, 2 * pr), 2 * pr)])
+            even = jnp.concatenate([t[:, :pr] for t in tiles], axis=1)
+            put(dst, p, jnp.where(odd, jnp.concatenate([t[:, pr:] for t in tiles], axis=1), even))
+
+    def put_other(dst, p, value):
+        dst[:, p * pr : (p + 2) * pr] = value
+
+    def put_own(dst, p, value):
+        dst[pl.ds(pl.multiple_of(c * tseq, tseq), tseq), p * pr : (p + 2) * pr] = value
+
+    my_rows = pl.ds(pl.multiple_of(c * tseq, tseq), tseq)
+    its_rows = pl.ds(pl.multiple_of((1 - c) * tseq, tseq), tseq)
+    load_x.wait()
+    pick(xin, xs, 1 - c, put_other)
+    key_xs = send(xs, xg.at[my_rows], sib)
+    load_y.wait()
+    pick(yin, ys, 1 - c, put_other)
+    key_ys = send(ys, yg.at[my_rows], sib)
     spread_done(*ab_keys)
     ga.start()
     gb.start()
-
-    load_x.wait()
-    load_y.wait()
-
-    def pick(src, dst, cc, put):
-        for p in range(0, CHIPS, 2):
-            got = []
-            for q in (p, p + 1):
-                shard = src[:, pl.ds(pl.multiple_of((2 * q + cc) * own, own), own)]
-                piece = shard[:, 0:pr]
-                for k in range(1, N_LAYER):
-                    piece = jnp.where(sx == k, shard[:, k * pr : (k + 1) * pr], piece)
-                got.append(piece)
-            put(dst, p, jnp.concatenate(got, axis=1))
-
-    def put_other(dst, p, value):
-        dst[:, p * pr : (p + 2) * pr] = value
-
-    def put_own(dst, p, value):
-        dst[pl.ds(pl.multiple_of(c * tseq, tseq), tseq), p * pr : (p + 2) * pr] = value
-
-    pick(xin, xs, 1 - c, put_other)
-    my_rows = pl.ds(pl.multiple_of(c * tseq, tseq), tseq)
-    its_rows = pl.ds(pl.multiple_of((1 - c) * tseq, tseq), tseq)
-    key_xs = send(xs, xg.at[my_rows], sib)
-    pick(yin, ys, 1 - c, put_other)
-    key_ys = send(ys, yg.at[my_rows], sib)
+    p_keys = spread((pbf.at[0], pbf.at[1]), (2, 3))
     pick(xin, xg, c, put_own)
     pick(yin, yg, c, put_own)
-
     ga.second()
     gb.second()
-
     xq = xin[pl.ds(pl.multiple_of(sx * tq, tq), tq), :].astype(f32)
     norm = jnp.sum(xq * xq, axis=1, keepdims=True)
     load_r.wait()
     res = res_ref[...]
     direc = dir_ref[...]
-
-    spread_done(*p_keys)
-    gpa.start()
-    gpb.start()
     arrive(key_xs, xg.at[its_rows])
     arrive(key_ys, yg.at[its_rows])
     xt[...] = xg[...].astype(f32).T.astype(bf16)
     yt[...] = yg[...].astype(f32).T.astype(bf16)
     ga.relay()
     gb.relay()
-    gpa.second()
-    gpb.second()
+    spread_done(*p_keys)
+    gpa.start()
+    gpb.start()
     ga.finish()
     gb.finish()
-
     wide = N_LAYER * rank
     wa = w[0].reshape(feats, wide)
     wb = w[1].reshape(feats, wide)
     xv = xg[...]
     yv = yg[...]
+    both_x = 2 * wide
     prod[:, 0:wide] = dot_nn(xv, wa)
-    prod[:, wide : 2 * wide] = dot_nn(xv, wb)
-    prod[:, 2 * wide : 3 * wide] = dot_nn(yv, wb)
-    prod_out[...] = prod[its_rows, :].astype(bf16)
-    key_prod = send(prod_out, prod_in, sib)
+    prod[:, wide:both_x] = dot_nn(xv, wb)
+    prod_out[:, 0:both_x] = prod[its_rows, 0:both_x].astype(bf16)
+    key_px = send(prod_out.at[:, 0:both_x], prod_in.at[:, 0:both_x], sib)
+    n_half = N_GRAM // 2
+    n_own = n_half // N_LAYER
     for j in range(N_LAYER):
         left = w[1, :, :, :, j * rank : (j + 1) * rank].reshape(feats, rank)
         if j < N_LAYER - 1:
@@ -281,52 +289,64 @@
         block = dot_tn(left, right)
         for l in range(j, N_LAYER):
             gram[SELF[(j, l)]] = block[:, (l - j) * rank : (l - j + 1) * rank]
-    n_half = N_GRAM // 2
     my_gram = pl.ds(c * n_half, n_half)
     gram_out[...] = gram[pl.ds((1 - c) * n_half, n_half)].astype(bf16)
     key_gram = send(gram_out, gram_in, sib)
-
-    arrive(key_prod, prod_in)
-    pair = prod[my_rows, :] + prod_in[...].astype(f32)
-    prod[my_rows, :] = pair
-    prodx_out[...] = pair.astype(bf16)
-    keys = []
-    for k in range(1, N_LAYER):
-        keys.append(send(rows(prodx_out, up(sx, k), tq), prodx_in.at[k - 1], line(k)))
+    prod[:, both_x:] = dot_nn(yv, wb)
+    prod_out[:, both_x:] = prod[its_rows, both_x:].astype(bf16)
+    key_py = send(prod_out.at[:, both_x:], prod_in.at[:, both_x:], sib)
+
+    def pair_sum(key, at):
+        arrive(key, prod_in.at[:, at])
+        pair = prod[my_rows, at] + prod_in[:, at].astype(f32)
+        prod[my_rows, at] = pair
+        prodx_out[:, at] = pair.astype(bf16)
+        keys = []
+        for k in (2, 1, 3):
+            src = prodx_out.at[pl.ds(pl.multiple_of(up(sx, k) * tq, tq), tq), at]
+            keys.append(send(src, prodx_in.at[k - 1, :, at], line(k)))
+        return keys
+
     arrive(key_gram, gram_in)
     gpair = gram[my_gram] + gram_in[...].astype(f32)
     gram[my_gram] = gpair
     gramx_out[...] = gpair.astype(bf16)
-    n_own = n_half // N_LAYER
     gkeys = []
-    for k in range(1, N_LAYER):
+    for k in (2, 1, 3):
         gkeys.append(send(gramx_out.at[pl.ds(up(sx, k) * n_own, n_own)], gramx_in.at[k - 1], line(k)))
-    gpa.relay()
-    gpb.relay()
-    gsum = gram[pl.ds(c * n_half + sx * n_own, n_own)]
-    for k in range(1, N_LAYER):
-        arrive(gkeys[k - 1], gramx_in.at[k - 1])
+    in_x, in_y = slice(0, both_x), slice(both_x, 3 * wide)
+    pxkeys = pair_sum(key_px, in_x)
+    pykeys = pair_sum(key_py, in_y)
+    gpa.second_direct()
+    gpb.second_direct()
+    mine = pl.ds(c * n_half + sx * n_own, n_own)
+    gsum = gram[mine]
+    for key, k in zip(gkeys, (2, 1, 3)):
+        arrive(key, gramx_in.at[k - 1])
         gsum = gsum + gramx_in[k - 1].astype(f32)
-    mine = pl.ds(c * n_half + sx * n_own, n_own)
     gfull[mine] = gsum.astype(bf16)
     gkeys = []
-    for k in range(1, N_LAYER):
+    for k in (2, 1, 3):
         gkeys.append(send(gfull.at[mine], gfull.at[mine], line(k)))
-    psum = prod[pl.ds(pl.multiple_of(c * tseq + sx * tq, tq), tq), :]
-    for k in range(1, N_LAYER):
-        arrive(keys[k - 1], prodx_in.at[k - 1])
-        psum = psum + prodx_in[k - 1].astype(f32)
-    for k in range(1, N_LAYER):
-        arrive(gkeys[k - 1], gfull.at[pl.ds(c * n_half + up(sx, -k) * n_own, n_own)])
+    token_rows = pl.ds(pl.multiple_of(c * tseq + sx * tq, tq), tq)
+
+    def line_sum(keys, at):
+        total = prod[token_rows, at]
+        for key, k in zip(keys, (2, 1, 3)):
+            arrive(key, prodx_in.at[k - 1, :, at])
+            total = total + prodx_in[k - 1, :, at].astype(f32)
+        return total
+
+    psum = line_sum(pxkeys, in_x)
+    for key, k in zip(gkeys, (2, 1, 3)):
+        arrive(key, gfull.at[pl.ds(c * n_half + up(sx, -k) * n_own, n_own)])
     key_gfull = send(gfull.at[my_gram], gfull.at[my_gram], sib)
     arrive(key_gfull, gfull.at[pl.ds((1 - c) * n_half, n_half)])
-
     def part(value, k):
         return value[:, k * rank : (k + 1) * rank]
 
     ha = [part(psum, l) for l in range(N_LAYER)]
     hb = [part(psum, N_LAYER + l) for l in range(N_LAYER)]
-    yb = [part(psum, 2 * N_LAYER + l) for l in range(N_LAYER)]
     acts, slopes, rhos, pres, hbs = [], [], [], [], []
     for l in range(N_LAYER):
         rho = jnp.sqrt(norm / width + norm_eps)
@@ -349,7 +369,13 @@
         slopes.append(sig * (1.0 + pre * (1.0 - sig)))
         rhos.append(rho)
         pres.append(pre)
-    cb = [hb[l] - yb[l] for l in range(N_LAYER)]
+    my_act = token_rows
+    a_cols, q_cols = slice(0, wide), slice(wide, 2 * wide + rank)
+    for l in range(N_LAYER):
+        act[my_act, l * rank : (l + 1) * rank] = acts[l]
+    akeys = [send(act.at[my_act, a_cols], act.at[my_act, a_cols], line(k)) for k in (2, 1, 3)]
+    ysum = line_sum(pykeys, in_y)
+    cb = [hb[l] - part(ysum, l) for l in range(N_LAYER)]
     qs = [None] * N_LAYER
     lane = lax.broadcasted_iota(jnp.int32, (tq, rank), 1)
     gains = jnp.zeros((tq, rank), f32)
@@ -361,20 +387,19 @@
             gains = jnp.where(lane == l, gain, gains)
             for j in range(l):
                 cb[j] = cb[j] + dot_nt(qs[l], gfull[CROSS[(j, l)]]) - gain * hbs[l][j]
-    my_act = pl.ds(pl.multiple_of(c * tseq + sx * tq, tq), tq)
     for l in range(N_LAYER):
-        act[my_act, l * rank : (l + 1) * rank] = acts[l]
         act[my_act, (N_LAYER + l) * rank : (N_LAYER + l + 1) * rank] = qs[l]
-    act[my_act, 2 * N_LAYER * rank :] = gains.astype(bf16)
-    keys = []
-    for k in range(1, N_LAYER):
-        keys.append(send(act.at[my_act], act.at[my_act], line(k)))
-    gpa.finish()
-    gpb.finish()
-    for k in range(1, N_LAYER):
-        arrive(keys[k - 1], act.at[pl.ds(pl.multiple_of(c * tseq + up(sx, -k) * tq, tq), tq)])
-    key_act = send(act.at[my_rows], act.at[my_rows], sib)
-    arrive(key_act, act.at[its_rows])
+    act[my_act, 2 * wide :] = gains.astype(bf16)
+    qkeys = [send(act.at[my_act, q_cols], act.at[my_act, q_cols], line(k)) for k in (2, 1, 3)]
+    sib_keys = []
+    for at, keys in ((a_cols, akeys), (q_cols, qkeys)):
+        for key, k in zip(keys, (2, 1, 3)):
+            arrive(key, act.at[pl.ds(pl.multiple_of(c * tseq + up(sx, -k) * tq, tq), tq), at])
+        sib_keys.append(send(act.at[my_rows, at], act.at[my_rows, at], sib))
+    gpa.finish_direct()
+    gpb.finish_direct()
+    for key, at in zip(sib_keys, (a_cols, q_cols)):
+        arrive(key, act.at[its_rows, at])
 
     av = [act[:, l * rank : (l + 1) * rank] for l in range(N_LAYER)]
     qv = [act[:, (N_LAYER + l) * rank : (N_LAYER + l + 1) * rank] for l in range(N_LAYER)]
@@ -579,7 +604,7 @@
         out_specs=(spec, spec),
         scratch_shapes=scratch,
         compiler_params=pltpu.CompilerParams(
-            collective_id=0, has_side_effects=True, vmem_limit_bytes=60 * 1024 * 1024
+            collective_id=0, has_side_effects=True, vmem_limit_bytes=52 * 1024 * 1024
         ),
         cost_estimate=pl.CostEstimate(flops=4_000_000_000, bytes_accessed=8_000_000, transcendentals=0),
     )(inputs, targets, down_proj[0], up_proj[0], direction[0], residual[0])

time: 107 us -> 99.3 us (0.928)
  Pallas kernels: 103 us -> 93.4 us
  local copies, waits for them, and re-layouts: 3.34 us -> 4.98 us
    pallas_call x1, Pallas kernels: 103 us -> 93.4 us  [step_kernel(): pl.pallas_call(kernel, out_shape=(out, out), in_specs=[hbm] * 6, out_spec...]
    unnamed x2 -> x10, local copies, waits for them, and re-layouts: 3.34 us -> 4.98 us
where the time goes in v3:
time: 99.3 us; the launch traced here: 99 us
  Pallas kernels  93.4 us (94%)
  local copies, waits for them, and re-layouts  4.98 us (5%)
    pallas_call x1, Pallas kernels, step_kernel(): pl.pallas_call(kernel, out_shape=(out, out), in_specs=[hbm] * 6, out_spec...  93.4 us
    unnamed x10, local copies, waits for them, and re-layouts  4.98 us

profile of v3, /device:TPU:1, one launch (start us, length us, event | category | flops | bytes accessed | tf_op | source)
XLA Modules:
  0.0 99.0 jit_solution(15763476492902132425)
XLA Ops:
  0.6 0.0 copy-start
  0.6 0.9 copy-done
  1.6 0.0 copy-start.1
  1.6 0.9 copy-done.1
  2.5 0.0 copy-start.2
  2.5 0.8 copy-done.2
  3.4 0.0 copy-start.3
  3.4 0.8 copy-done.3
  4.2 93.4 %shard_map.77 = (f32[2,256,128]{2,1,0:T(8,128)S(1)}, f32[2,256,128]{2,1,0:T(8,128)S(1)}) custom-call(bf16[128,8192]{1,0:T(8,128)(2,1)} %x_hbm.1, bf16[128,8192]{1,0:T(8,128)(2,1)} %y_hbm.1, bf16[256,128]{1,0:T(8,128)(2,1)S(1)} %bitcast.10, bf16[256,128]{1,0:T(8,128)(2,1)S(1)} %bitcast.11, f32[2,256,128]{2,1,0:T(8,128)S(1)} %bitcast.8, f32[2,256,128]{2,1,0:T(8,128)S(1)} %bitcast.9), custom_call_target="tpu_custom_call" | custom-call | flops 4000000000 | bytes 8000000 | tf_op jit(solution)/shard_map/pallas_call | solution.py:600
  97.6 0.7 copy.10
  98.3 0.7 copy.11
Async XLA Ops:
  0.6 1.0 copy-start
  1.6 0.9 copy-start.1
  2.5 0.8 copy-start.2
  3.4 0.8 copy-start.3

commit v4 on v3

--- a/solution.py
+++ b/solution.py
@@ -49,15 +49,15 @@
         return self.n - 1
 
 
-N_SEM = 125
+N_SEM = 148
 
 
 def kernel(
     x_hbm, y_hbm, a_ref, b_ref, dir_hbm, res_hbm,
-    newres_ref, newdir_ref,
+    big_hbm, coef_ref,
     xin, yin, dir_ref, res_ref, xg, yg, xs, ys, xt, yt, w, pbf,
     prod, prod_out, prod_in, prodx_out, prodx_in,
-    gram, gram_out, gram_in, gramx_out, gramx_in, gfull,
+    gram, gram_out, gram_in, gramx_out, gramx_in, gline_out, gline_in, gfull, res_s, big_vmem,
     act, ht, g, pair_in, acc2, block_in, fin,
     gx, stat_out, stat_in, stat2_out, stat2_in, dv_out, dv_in,
     send_sem, recv_sem, local_sem,
@@ -82,10 +82,14 @@
         return (yy * SIDE + zz) * 2 + cc
 
     barrier = pltpu.get_barrier_semaphore()
-    for k in range(1, 8):
-        px = up(sx, k // 2)
-        pc = lax.rem(c + k, 2)
-        pl.semaphore_signal(barrier, inc=1, device_id=(px, fs(y, z, pc)), device_id_type=MESH)
+    sib = (sx, fs(y, z, 1 - c))
+
+    def line(k):
+        return (up(sx, k), f)
+
+    for k in range(1, N_LAYER):
+        pl.semaphore_signal(barrier, inc=1, device_id=line(k), device_id_type=MESH)
+    pl.semaphore_signal(barrier, inc=1, device_id=sib, device_id_type=MESH)
     for k in range(1, SIDE):
         pl.semaphore_signal(barrier, inc=1, device_id=(sx, fs(up(y, k), z, c)), device_id_type=MESH)
         pl.semaphore_signal(barrier, inc=1, device_id=(sx, fs(y, up(z, k), c)), device_id_type=MESH)
@@ -101,7 +105,7 @@
     load_d.wait()
     pbf[...] = dir_ref[...].astype(bf16)
 
-    pl.semaphore_wait(barrier, 7 + 2 * (SIDE - 1))
+    pl.semaphore_wait(barrier, 1 + 3 * (SIDE - 1))
 
     counter = Counter()
     pending = []
@@ -122,13 +126,11 @@
             device_id=(sx, f), device_id_type=MESH,
         ).wait_recv()
 
-    sib = (sx, fs(y, z, 1 - c))
-
-    def line(k):
-        return (up(sx, k), f)
-
     def rows(ref, at, size):
         return ref.at[pl.ds(pl.multiple_of(at * size, size), size)]
+
+    def rows2(ref, at):
+        return ref.at[:, pl.ds(pl.multiple_of(at * pr, pr), pr)]
 
     def cols(at):
         return pl.ds(pl.multiple_of(at * rank, rank), rank)
@@ -245,23 +247,81 @@
     spread_done(*ab_keys)
     ga.start()
     gb.start()
-    p_keys = spread((pbf.at[0], pbf.at[1]), (2, 3))
+    p_keys = [send(rows2(pbf, up(sx, k)), w.at[2:4, y, z, :, cols(sx)], line(k)) for k in (2, 1, 3)]
+    copy_p = pltpu.make_async_copy(rows2(pbf, sx), w.at[2:4, y, z, :, cols(sx)], local_sem.at[4])
+    copy_p.start()
+    half_rows = rank // 2
+    mine_a, mine_b = w[0, y, z], w[1, y, z]
+    for j in range(N_LAYER):
+        left = mine_b[:, j * rank : (j + 1) * rank]
+        if j < N_LAYER - 1:
+            block = dot_tn(left, mine_a[:, (j + 1) * rank :])
+            for l in range(j + 1, N_LAYER):
+                b = CROSS[(j, l)]
+                gram[2 * b : 2 * b + 2] = block[:, (l - j - 1) * rank : (l - j) * rank].reshape(2, half_rows, rank)
+        block = dot_tn(left, mine_b[:, j * rank :])
+        for l in range(j, N_LAYER):
+            b = SELF[(j, l)]
+            gram[2 * b : 2 * b + 2] = block[:, (l - j) * rank : (l - j + 1) * rank].reshape(2, half_rows, rank)
+    my_gram = pl.ds(c * CHIPS, CHIPS)
+    its_gram = pl.ds((1 - c) * CHIPS, CHIPS)
+    gram_out[...] = gram[its_gram].astype(bf16)
+    key_gram = send(gram_out, gram_in, sib)
     pick(xin, xg, c, put_own)
     pick(yin, yg, c, put_own)
+    arrive(key_gram, gram_in)
+    gpair = gram[my_gram] + gram_in[...].astype(f32)
+    gram[my_gram] = gpair
+    gramx_out[...] = gpair.astype(bf16)
+
+    def chip(k):
+        return up(y, k // SIDE) * SIDE + up(z, k % SIDE)
+
+    def chip_dev(k):
+        return (sx, fs(up(y, k // SIDE), up(z, k % SIDE), c))
+
+    def chip_back(k):
+        return up(y, -(k // SIDE)) * SIDE + up(z, -(k % SIDE))
+
     ga.second()
     gb.second()
+    gkeys = [send(gramx_out.at[chip(k)], gramx_in.at[k - 1], chip_dev(k)) for k in range(1, CHIPS)]
     xq = xin[pl.ds(pl.multiple_of(sx * tq, tq), tq), :].astype(f32)
     norm = jnp.sum(xq * xq, axis=1, keepdims=True)
     load_r.wait()
     res = res_ref[...]
     direc = dir_ref[...]
+
+    def fold_home(v):
+        return jnp.sum(v.reshape(-1, rank), axis=0, keepdims=True)
+
+    dd = fold_home(direc * direc)
+    home = jnp.concatenate(
+        [fold_home(res * res), dd, fold_home(res * direc), dd, jnp.zeros((4, rank), f32)], axis=0
+    )
     arrive(key_xs, xg.at[its_rows])
     arrive(key_ys, yg.at[its_rows])
     xt[...] = xg[...].astype(f32).T.astype(bf16)
     yt[...] = yg[...].astype(f32).T.astype(bf16)
+    my_piece = c * CHIPS + y * SIDE + z
+    gsum = gram[my_piece]
+    for k in range(1, CHIPS):
+        arrive(gkeys[k - 1], gramx_in.at[k - 1])
+        gsum = gsum + gramx_in[k - 1].astype(f32)
+    gline_out[...] = gsum.astype(bf16)
+    gkeys = [send(gline_out, gline_in.at[k - 1], line(k)) for k in (2, 1, 3)]
     ga.relay()
     gb.relay()
-    spread_done(*p_keys)
+    for key, k in zip(gkeys, (2, 1, 3)):
+        arrive(key, gline_in.at[k - 1])
+        gsum = gsum + gline_in[k - 1].astype(f32)
+    gfull[my_piece] = gsum.astype(bf16)
+    gkeys = [send(gfull.at[my_piece], gfull.at[my_piece], chip_dev(k)) for k in range(1, CHIPS)]
+    res_keys = [send(rows2(res_ref, up(sx, k)), res_s.at[:, :, cols(sx)], line(k)) for k in (2, 1, 3)]
+    res_s[:, :, cols(sx)] = res_ref[:, pl.ds(pl.multiple_of(sx * pr, pr), pr)]
+    copy_p.wait()
+    for key, k in zip(p_keys, (2, 1, 3)):
+        arrive(key, w.at[2:4, y, z, :, cols(up(sx, -k))])
     gpa.start()
     gpb.start()
     ga.finish()
@@ -276,22 +336,6 @@
     prod[:, wide:both_x] = dot_nn(xv, wb)
     prod_out[:, 0:both_x] = prod[its_rows, 0:both_x].astype(bf16)
     key_px = send(prod_out.at[:, 0:both_x], prod_in.at[:, 0:both_x], sib)
-    n_half = N_GRAM // 2
-    n_own = n_half // N_LAYER
-    for j in range(N_LAYER):
-        left = w[1, :, :, :, j * rank : (j + 1) * rank].reshape(feats, rank)
-        if j < N_LAYER - 1:
-            right = w[0, :, :, :, (j + 1) * rank : wide].reshape(feats, wide - (j + 1) * rank)
-            block = dot_tn(left, right)
-            for l in range(j + 1, N_LAYER):
-                gram[CROSS[(j, l)]] = block[:, (l - j - 1) * rank : (l - j) * rank]
-        right = w[1, :, :, :, j * rank : wide].reshape(feats, wide - j * rank)
-        block = dot_tn(left, right)
-        for l in range(j, N_LAYER):
-            gram[SELF[(j, l)]] = block[:, (l - j) * rank : (l - j + 1) * rank]
-    my_gram = pl.ds(c * n_half, n_half)
-    gram_out[...] = gram[pl.ds((1 - c) * n_half, n_half)].astype(bf16)
-    key_gram = send(gram_out, gram_in, sib)
     prod[:, both_x:] = dot_nn(yv, wb)
     prod_out[:, both_x:] = prod[its_rows, both_x:].astype(bf16)
     key_py = send(prod_out.at[:, both_x:], prod_in.at[:, both_x:], sib)
@@ -307,27 +351,14 @@
             keys.append(send(src, prodx_in.at[k - 1, :, at], line(k)))
         return keys
 
-    arrive(key_gram, gram_in)
-    gpair = gram[my_gram] + gram_in[...].astype(f32)
-    gram[my_gram] = gpair
-    gramx_out[...] = gpair.astype(bf16)
-    gkeys = []
-    for k in (2, 1, 3):
-        gkeys.append(send(gramx_out.at[pl.ds(up(sx, k) * n_own, n_own)], gramx_in.at[k - 1], line(k)))
     in_x, in_y = slice(0, both_x), slice(both_x, 3 * wide)
     pxkeys = pair_sum(key_px, in_x)
     pykeys = pair_sum(key_py, in_y)
+    for k in range(1, CHIPS):
+        arrive(gkeys[k - 1], gfull.at[c * CHIPS + chip_back(k)])
+    key_gfull = send(gfull.at[my_gram], gfull.at[my_gram], sib)
     gpa.second_direct()
     gpb.second_direct()
-    mine = pl.ds(c * n_half + sx * n_own, n_own)
-    gsum = gram[mine]
-    for key, k in zip(gkeys, (2, 1, 3)):
-        arrive(key, gramx_in.at[k - 1])
-        gsum = gsum + gramx_in[k - 1].astype(f32)
-    gfull[mine] = gsum.astype(bf16)
-    gkeys = []
-    for k in (2, 1, 3):
-        gkeys.append(send(gfull.at[mine], gfull.at[mine], line(k)))
     token_rows = pl.ds(pl.multiple_of(c * tseq + sx * tq, tq), tq)
 
     def line_sum(keys, at):
@@ -338,10 +369,11 @@
         return total
 
     psum = line_sum(pxkeys, in_x)
-    for key, k in zip(gkeys, (2, 1, 3)):
-        arrive(key, gfull.at[pl.ds(c * n_half + up(sx, -k) * n_own, n_own)])
-    key_gfull = send(gfull.at[my_gram], gfull.at[my_gram], sib)
-    arrive(key_gfull, gfull.at[pl.ds((1 - c) * n_half, n_half)])
+    arrive(key_gfull, gfull.at[its_gram])
+
+    def gblock(b):
+        return gfull[2 * b : 2 * b + 2].reshape(rank, rank)
+
     def part(value, k):
         return value[:, k * rank : (k + 1) * rank]
 
@@ -356,13 +388,13 @@
         hbs.append(hb[:l])
         before = hb[l]
         for m in range(l + 1, N_LAYER):
-            ha[m] = ha[m] + dot_nn(a, gfull[CROSS[(l, m)]])
+            ha[m] = ha[m] + dot_nn(a, gblock(CROSS[(l, m)]))
         nxt = []
         for m in range(N_LAYER):
             if l <= m:
-                nxt.append(hb[m] + dot_nn(a, gfull[SELF[(l, m)]]))
+                nxt.append(hb[m] + dot_nn(a, gblock(SELF[(l, m)])))
             else:
-                nxt.append(hb[m] + dot_nt(a, gfull[SELF[(m, l)]]))
+                nxt.append(hb[m] + dot_nt(a, gblock(SELF[(m, l)])))
         hb = nxt
         norm = norm + jnp.sum(a.astype(f32) * (before + hb[l]), axis=1, keepdims=True)
         acts.append(a)
@@ -386,54 +418,61 @@
             gain = jnp.sum(cot * pres[l], axis=1, keepdims=True) / (width * rhos[l] * rhos[l])
             gains = jnp.where(lane == l, gain, gains)
             for j in range(l):
-                cb[j] = cb[j] + dot_nt(qs[l], gfull[CROSS[(j, l)]]) - gain * hbs[l][j]
+                cb[j] = cb[j] + dot_nt(qs[l], gblock(CROSS[(j, l)])) - gain * hbs[l][j]
     for l in range(N_LAYER):
         act[my_act, (N_LAYER + l) * rank : (N_LAYER + l + 1) * rank] = qs[l]
     act[my_act, 2 * wide :] = gains.astype(bf16)
     qkeys = [send(act.at[my_act, q_cols], act.at[my_act, q_cols], line(k)) for k in (2, 1, 3)]
-    sib_keys = []
-    for at, keys in ((a_cols, akeys), (q_cols, qkeys)):
+    def share(keys, at):
         for key, k in zip(keys, (2, 1, 3)):
             arrive(key, act.at[pl.ds(pl.multiple_of(c * tseq + up(sx, -k) * tq, tq), tq), at])
-        sib_keys.append(send(act.at[my_rows, at], act.at[my_rows, at], sib))
+        return send(act.at[my_rows, at], act.at[my_rows, at], sib)
+
+    key = share(akeys, a_cols)
+    arrive(key, act.at[its_rows, a_cols])
+
+    def wq(arr, l, q):
+        return w[arr, q, :, :, l * rank : (l + 1) * rank].reshape(quad, rank)
+
+    av = [act[:, l * rank : (l + 1) * rank] for l in range(N_LAYER)]
+    for q in range(SIDE):
+        fr = slice(q * quad, (q + 1) * quad)
+        h = xt[fr, :].astype(f32)
+        for l in range(N_LAYER):
+            hb16 = h.astype(bf16)
+            ht[l, fr, :] = hb16
+            h = hb16.astype(f32) + dot_nt(wq(1, l, q), av[l])
+        ht[2 * N_LAYER - 1, fr, :] = (h - yt[fr, :].astype(f32)).astype(bf16)
+    key = share(qkeys, q_cols)
     gpa.finish_direct()
     gpb.finish_direct()
-    for key, at in zip(sib_keys, (a_cols, q_cols)):
-        arrive(key, act.at[its_rows, at])
-
-    av = [act[:, l * rank : (l + 1) * rank] for l in range(N_LAYER)]
+    arrive(key, act.at[its_rows, q_cols])
     qv = [act[:, (N_LAYER + l) * rank : (N_LAYER + l + 1) * rank] for l in range(N_LAYER)]
     gain_t = act[:, 2 * N_LAYER * rank :].astype(f32).T
     d0 = jnp.zeros((quad, rank), f32)
     d1 = jnp.zeros((quad, rank), f32)
     for q in range(SIDE):
         fr = slice(q * quad, (q + 1) * quad)
-
-        def wq(arr, l):
-            return w[arr, q, :, :, l * rank : (l + 1) * rank].reshape(quad, rank)
-
-        h = xt[fr, :].astype(f32)
-        hs = []
-        for l in range(N_LAYER):
-            hb16 = h.astype(bf16)
-            hs.append(hb16)
-            ht[l, fr, :] = hb16
-            h = hb16.astype(f32) + dot_nt(wq(1, l), av[l])
-        cot = (h - yt[fr, :].astype(f32)).astype(bf16)
+        cot = ht[2 * N_LAYER - 1, fr, :]
         for l in range(N_LAYER - 1, -1, -1):
-            ht[N_LAYER + l, fr, :] = cot
-            for arr, left, right in ((2, hs[l], qv[l]), (3, cot, av[l])):
-                pw = wq(arr, l).astype(f32)
+            hl = ht[l, fr, :]
+            for arr, left, right in ((2, hl, qv[l]), (3, cot, av[l])):
+                pw = wq(arr, l, q).astype(f32)
                 d0 = d0 + dot_nn(left[:, :tseq], right[:tseq]) * pw
                 d1 = d1 + dot_nn(left[:, tseq:], right[tseq:]) * pw
             if l > 0:
                 cot = (
-                    cot.astype(f32) + dot_nt(wq(0, l), qv[l]) - gain_t[l : l + 1, :] * hs[l].astype(f32)
+                    cot.astype(f32) + dot_nt(wq(0, l, q), qv[l]) - gain_t[l : l + 1, :] * hl.astype(f32)
                 ).astype(bf16)
+                ht[N_LAYER + l - 1, fr, :] = cot
+
     def fold(v):
-        return jnp.sum(v.reshape(quad // 8, 8, rank), axis=0)
-
-    dv_out[...] = jnp.concatenate([fold(d0), fold(d1)], axis=0)
+        return jnp.sum(v.reshape(-1, rank), axis=0, keepdims=True)
+
+    def stack(values):
+        return jnp.concatenate([fold(v) for v in values] + [jnp.zeros((8 - len(values), rank), f32)], axis=0)
+
+    dv_out[...] = stack([d0, d1])
     keys = []
     for k in range(1, 8):
         keys.append(send(dv_out, dv_in.at[k - 1], (up(sx, k // 2), fs(y, z, lax.rem(c + k, 2)))))
@@ -441,14 +480,14 @@
     for k in range(1, 8):
         arrive(keys[k - 1], dv_in.at[k - 1])
         dv = dv + dv_in[k - 1]
-    s0 = jnp.sum(dv[:8], keepdims=True) / (tseq * width)
-    s1 = jnp.sum(dv[8:], keepdims=True) / (tseq * width)
+    s0 = jnp.sum(dv[0:1], keepdims=True) / (tseq * width)
+    s1 = jnp.sum(dv[1:2], keepdims=True) / (tseq * width)
     token = lax.broadcasted_iota(jnp.int32, (2 * tseq, 1), 0)
     scale = jnp.where(token < tseq, s0, s1)
     qd = [(qv[l].astype(f32) * scale).astype(bf16) for l in range(N_LAYER)]
     ad = [(av[l].astype(f32) * scale).astype(bf16) for l in range(N_LAYER)]
 
-    for arr, base, right in ((0, 0, qd), (1, N_LAYER, ad)):
+    def gradient(arr, base, right):
         for l in range(N_LAYER):
             for q in range(SIDE):
                 value = dot_nn(ht[base + l, q * quad : (q + 1) * quad, :], right[l])
@@ -503,6 +542,7 @@
             for i in (1, -1, 2):
                 arrive(self.key[("s", i)], block_in.at[self.arr, i % SIDE - 1])
                 value = value + block_in[self.arr, i % SIDE - 1].astype(f32)
+            self.value = value
             fin[self.arr, SIDE] = value.astype(bf16)
             self.back = []
             for k in range(1, N_LAYER):
@@ -515,26 +555,33 @@
                 arrive(self.back[k - 1], gx.at[self.arr, up(sx, -k)])
 
     both = (Scatter(0, "y"), Scatter(1, "z"))
-    for s in both:
-        s.start()
+    gradient(0, 0, qd)
+    both[0].start()
+    gradient(1, N_LAYER, ad)
+    both[1].start()
     for s in both:
         s.middle()
     for s in both:
         s.end()
     for s in both:
         s.end2()
-    for s in both:
-        s.done()
-
     tokens_total = tseq * 2 * CHIPS
     shrink = 1.0 / (damping * tokens_total * width)
-    grad = gx[...].astype(f32).reshape(2, own, rank)
-    big = grad * shrink + direc
-
-    def fold2(v):
-        return jnp.sum(v.reshape(2 * own // 8, 8, rank), axis=0)
-
-    stat_out[...] = jnp.concatenate([fold2(res * res), fold2(direc * big), fold2(res * big), fold2(big * big)], axis=0)
+
+    def lanes(v):
+        return sum(v[:, l * rank : (l + 1) * rank] for l in range(N_LAYER))
+
+    pg = rg = gg = 0.0
+    for key, k in zip(res_keys, (2, 1, 3)):
+        arrive(key, res_s.at[:, :, cols(up(sx, -k))])
+    for s in both:
+        pg = pg + lanes(s.value * w[2 + s.arr, y, z].astype(f32))
+        rg = rg + lanes(s.value * res_s[s.arr])
+        gg = gg + lanes(s.value * s.value)
+    pg, rg, gg = fold(pg) * shrink, fold(rg) * shrink, fold(gg) * (shrink * shrink)
+    stat_out[...] = home + jnp.concatenate(
+        [jnp.zeros((1, rank), f32), pg, rg, 2.0 * pg + gg, jnp.zeros((4, rank), f32)], axis=0
+    )
     keys = []
     for k in range(1, 8):
         keys.append(send(stat_out, stat_in.at[k - 1], (up(sx, k // 2), fs(y, z, lax.rem(c + k, 2)))))
@@ -543,22 +590,24 @@
         arrive(keys[k - 1], stat_in.at[k - 1])
         total = total + stat_in[k - 1]
     stat2_out[...] = total
-    keys = []
-    for k in range(1, CHIPS):
-        keys.append(send(stat2_out, stat2_in.at[k - 1], (sx, fs(up(y, k // SIDE), up(z, k % SIDE), c))))
+    keys = [send(stat2_out, stat2_in.at[k - 1], chip_dev(k)) for k in range(1, CHIPS)]
+    for s in both:
+        s.done()
+    big_vmem[...] = gx[...].astype(f32).reshape(2, own, rank) * shrink + direc
+    copy_big = pltpu.make_async_copy(big_vmem, big_hbm, local_sem.at[5])
+    copy_big.start()
     for k in range(1, CHIPS):
         arrive(keys[k - 1], stat2_in.at[k - 1])
         total = total + stat2_in[k - 1]
-    rr = jnp.sum(total[0:8], keepdims=True)
-    pq = jnp.sum(total[8:16], keepdims=True) * damping
-    rp = jnp.sum(total[16:24], keepdims=True)
-    pp = jnp.sum(total[24:32], keepdims=True)
+    rr = jnp.sum(total[0:1], keepdims=True)
+    pq = jnp.sum(total[1:2], keepdims=True) * damping
+    rp = jnp.sum(total[2:3], keepdims=True)
+    pp = jnp.sum(total[3:4], keepdims=True)
     step = rr / pq * damping
     norm_new = rr - 2.0 * (step * rp) + step * (step * pp)
-    beta = norm_new / rr
-    new_res = res - step * big
-    newres_ref[...] = new_res
-    newdir_ref[...] = new_res + beta * direc
+    row = lax.broadcasted_iota(jnp.int32, (8, rank), 0)
+    coef_ref[...] = jnp.where(row == 0, step, norm_new / rr)
+    copy_big.wait()
     for copy in pending:
         copy.wait_send()
 
@@ -570,8 +619,7 @@
     feats = CHIPS * pr
     tq = tseq // N_LAYER
     wide = N_LAYER * rank
-    n_half = N_GRAM // 2
-    n_own = n_half // N_LAYER
+    hr = rank // 2
     vm = pltpu.VMEM
     scratch = [
         vm((tseq, width), bf16), vm((tseq, width), bf16),
@@ -582,32 +630,34 @@
         vm((4, SIDE, SIDE, pr, wide), bf16), vm((2, own, rank), bf16),
         vm((2 * tseq, 3 * wide), f32), vm((tseq, 3 * wide), bf16), vm((tseq, 3 * wide), bf16),
         vm((tseq, 3 * wide), bf16), vm((N_LAYER - 1, tq, 3 * wide), bf16),
-        vm((N_GRAM, rank, rank), f32), vm((n_half, rank, rank), bf16), vm((n_half, rank, rank), bf16),
-        vm((n_half, rank, rank), bf16), vm((N_LAYER - 1, n_own, rank, rank), bf16), vm((N_GRAM, rank, rank), bf16),
+        vm((2 * CHIPS, hr, rank), f32), vm((CHIPS, hr, rank), bf16), vm((CHIPS, hr, rank), bf16),
+        vm((CHIPS, hr, rank), bf16), vm((CHIPS - 1, hr, rank), bf16), vm((hr, rank), bf16),
+        vm((N_LAYER - 1, hr, rank), bf16), vm((2 * CHIPS, hr, rank), bf16),
+        vm((2, pr, wide), f32), vm((2, own, rank), f32),
         vm((2 * tseq, 2 * wide + rank), bf16), vm((2 * N_LAYER, feats, 2 * tseq), bf16),
         vm((2, SIDE, SIDE, pr, wide), bf16),
         vm((2, 6, 2, pr, wide), bf16),
         vm((2, SIDE, pr, wide), f32),
         vm((2, 3, pr, wide), bf16), vm((2, SIDE + 1, pr, wide), bf16),
         vm((2, N_LAYER, pr, rank), bf16),
-        vm((32, rank), f32), vm((7, 32, rank), f32), vm((32, rank), f32), vm((CHIPS - 1, 32, rank), f32),
-        vm((16, rank), f32), vm((7, 16, rank), f32),
+        vm((8, rank), f32), vm((7, 8, rank), f32), vm((8, rank), f32), vm((CHIPS - 1, 8, rank), f32),
+        vm((8, rank), f32), vm((7, 8, rank), f32),
         pltpu.SemaphoreType.DMA((N_SEM,)), pltpu.SemaphoreType.DMA((N_SEM,)), pltpu.SemaphoreType.DMA((8,)),
     ]
-    spec = pl.BlockSpec(memory_space=pltpu.VMEM)
     hbm = pl.BlockSpec(memory_space=pl.ANY)
-    out = jax.ShapeDtypeStruct((2, own, rank), f32)
-    new_res, new_dir = pl.pallas_call(
+    big, coef = pl.pallas_call(
         kernel,
-        out_shape=(out, out),
+        out_shape=(jax.ShapeDtypeStruct((2, own, rank), f32), jax.ShapeDtypeStruct((8, rank), f32)),
         in_specs=[hbm] * 6,
-        out_specs=(spec, spec),
+        out_specs=(hbm, pl.BlockSpec(memory_space=pltpu.VMEM)),
         scratch_shapes=scratch,
         compiler_params=pltpu.CompilerParams(
-            collective_id=0, has_side_effects=True, vmem_limit_bytes=52 * 1024 * 1024
+            collective_id=0, has_side_effects=True, vmem_limit_bytes=58 * 1024 * 1024
         ),
         cost_estimate=pl.CostEstimate(flops=4_000_000_000, bytes_accessed=8_000_000, transcendentals=0),
     )(inputs, targets, down_proj[0], up_proj[0], direction[0], residual[0])
+    new_res = residual[0] - coef[0, 0] * big
+    new_dir = new_res + coef[1, 0] * direction[0]
     return new_res[None], new_dir[None]
 
 

time: 99.3 us -> 89.2 us (0.90)
  Pallas kernels: 93.4 us -> 83.9 us
  local copies, waits for them, and re-layouts: 4.98 us -> 1.31 us
  other arithmetic: 0 us -> 3.04 us
    pallas_call x1, Pallas kernels: 93.4 us -> 83.9 us  [step_kernel(): pl.pallas_call(kernel, out_shape=(jax.ShapeDtypeStruct((2, own, rank), f3...]
    unnamed x10 -> x4, local copies, waits for them, and re-layouts: 4.98 us -> 0.01 us
    broadcast_in_dim x0 -> x1, other arithmetic: none -> 3.04 us  [step_kernel(): return (new_res[None], new_dir[None])]
    slice x0 -> x1, local copies, waits for them, and re-layouts: none -> 1.3 us  [step_kernel(): new_dir = new_res + coef[1, 0] * direction[0]]
where the time goes in v4:
time: 89.2 us; the launch traced here: 88.9 us
  Pallas kernels  83.9 us (94%)
  other arithmetic  3.04 us (3%)
  local copies, waits for them, and re-layouts  1.31 us (1%)
    pallas_call x1, Pallas kernels, step_kernel(): pl.pallas_call(kernel, out_shape=(jax.ShapeDtypeStruct((2, own, rank), f3...  83.9 us
    broadcast_in_dim x1, other arithmetic, step_kernel(): return (new_res[None], new_dir[None])  3.04 us

profile of v4, /device:TPU:1, one launch (start us, length us, event | category | flops | bytes accessed | tf_op | source)
XLA Modules:
  0.0 88.9 jit_solution(1642669985513254160)
XLA Ops:
  0.6 0.0 copy-start
  0.6 0.0 copy-start.1
  0.7 83.9 %shard_map.77 = (f32[2,256,128]{2,1,0:T(8,128)}, f32[8,128]{1,0:T(8,128)}) custom-call(bf16[128,8192]{1,0:T(8,128)(2,1)} %x_hbm.1, bf16[128,8192]{1,0:T(8,128)(2,1)} %y_hbm.1, bf16[256,128]{1,0:T(8,128)(2,1)} %bitcast.15, bf16[256,128]{1,0:T(8,128)(2,1)} %bitcast.16, f32[2,256,128]{2,1,0:T(8,128)} %bitcast.13, f32[2,256,128]{2,1,0:T(8,128)} %bitcast.14), custom_call_target="tpu_custom_call" | custom-call | flops 4000000000 | bytes 8000000 | tf_op jit(solution)/shard_map/pallas_call | solution.py:648
  84.6 1.3 %fusion.1 = (f32[1,1]{1,0:T(1,128)}, f32[1,1]{1,0:T(1,128)}) fusion(f32[8,128]{1,0:T(8,128)} %get-tuple-element.4), kind=kLoop, calls=%fused_computation.3 | loop fusion | bytes 16 | tf_op jit(solution)/shard_map/slice | solution.py:660
  85.9 0.0 copy-done
  85.9 0.0 copy-done.1
  85.9 3.0 %add_bitcast_fusion = (f32[1,2,256,128]{3,2,1,0:T(8,128)}, f32[1,2,256,128]{3,2,1,0:T(8,128)}) fusion(f32[]{:T(128)} %bitcast.6, f32[2,256,128]{2,1,0:T(8,128)} %get-tuple-element.5, f32[]{:T(128)} %bitcast.4, f32[1,2,256,128]{3,2,1,0:T(8,128)S(1)} %copy-done, f32[1,2,256,128]{3,2,1,0:T(8,128)S(1)} %copy-done.1), kind=kLoop, calls=%fused_computation | loop fusion | flops 262144 | bytes 1310728 | tf_op jit(solution)/shard_map/broadcast_in_dim | solution.py:661
Async XLA Ops:
  0.6 85.2 %copy-start = (f32[1,2,256,128]{3,2,1,0:T(8,128)S(1)}, f32[1,2,256,128]{3,2,1,0:T(8,128)}, u32[]{:S(2)}) copy-start(f32[1,2,256,128]{3,2,1,0:T(8,128)} %param.10) | copy-start | bytes 786436
  0.6 85.2 %copy-start.1 = (f32[1,2,256,128]{3,2,1,0:T(8,128)S(1)}, f32[1,2,256,128]{3,2,1,0:T(8,128)}, u32[]{:S(2)}) copy-start(f32[1,2,256,128]{3,2,1,0:T(8,128)} %param.11) | copy-start | bytes 786436

commit v5 on v4

--- a/solution.py
+++ b/solution.py
@@ -49,15 +49,15 @@
         return self.n - 1
 
 
-N_SEM = 148
+N_SEM = 154
 
 
 def kernel(
     x_hbm, y_hbm, a_ref, b_ref, dir_hbm, res_hbm,
-    big_hbm, coef_ref,
+    newres_ref, newdir_ref,
     xin, yin, dir_ref, res_ref, xg, yg, xs, ys, xt, yt, w, pbf,
     prod, prod_out, prod_in, prodx_out, prodx_in,
-    gram, gram_out, gram_in, gramx_out, gramx_in, gline_out, gline_in, gfull, res_s, big_vmem,
+    gram, gram_out, gram_in, gramx_out, gramx_in, gline_out, gline_in, gfull, res_s,
     act, ht, g, pair_in, acc2, block_in, fin,
     gx, stat_out, stat_in, stat2_out, stat2_in, dv_out, dv_in,
     send_sem, recv_sem, local_sem,
@@ -102,8 +102,6 @@
     load_x.start()
     load_y.start()
     load_r.start()
-    load_d.wait()
-    pbf[...] = dir_ref[...].astype(bf16)
 
     pl.semaphore_wait(barrier, 1 + 3 * (SIDE - 1))
 
@@ -157,6 +155,8 @@
             arrive(key, w.at[arr, y, z, :, cols(up(sx, -k))])
 
     ab_keys = spread((a_ref, b_ref), (0, 1))
+    load_d.wait()
+    pbf[...] = dir_ref[...].astype(bf16)
 
     class Gather:
         def __init__(self, arr, first):
@@ -182,21 +182,6 @@
         def start(self):
             for i in (2, 1, -1):
                 self.push(i, self.block(0), i, 0)
-
-        def second_direct(self):
-            for i in (1, -1, 2):
-                arrive(self.key[i], self.block(-i))
-            for j in (2, 1, -1):
-                self.key[("d", j)] = send(self.whole(0), self.whole(0), self.dev(0, j))
-
-        def finish_direct(self):
-            for j in (1, -1, 2):
-                arrive(self.key[("d", j)], self.whole(-j))
-
-        def whole(self, j):
-            if self.first == "y":
-                return w.at[self.arr, :, up(z, j)]
-            return w.at[self.arr, up(y, j)]
 
         def second(self):
             for i in (1, -1, 2):
@@ -303,6 +288,15 @@
     arrive(key_ys, yg.at[its_rows])
     xt[...] = xg[...].astype(f32).T.astype(bf16)
     yt[...] = yg[...].astype(f32).T.astype(bf16)
+    ga.relay()
+    gb.relay()
+    copy_p.wait()
+    for key, k in zip(p_keys, (2, 1, 3)):
+        arrive(key, w.at[2:4, y, z, :, cols(up(sx, -k))])
+    gpa.start()
+    gpb.start()
+    res_keys = [send(rows2(res_ref, up(sx, k)), res_s.at[:, :, cols(sx)], line(k)) for k in (2, 1, 3)]
+    res_s[:, :, cols(sx)] = res_ref[:, pl.ds(pl.multiple_of(sx * pr, pr), pr)]
     my_piece = c * CHIPS + y * SIDE + z
     gsum = gram[my_piece]
     for k in range(1, CHIPS):
@@ -310,22 +304,9 @@
         gsum = gsum + gramx_in[k - 1].astype(f32)
     gline_out[...] = gsum.astype(bf16)
     gkeys = [send(gline_out, gline_in.at[k - 1], line(k)) for k in (2, 1, 3)]
-    ga.relay()
-    gb.relay()
-    for key, k in zip(gkeys, (2, 1, 3)):
-        arrive(key, gline_in.at[k - 1])
-        gsum = gsum + gline_in[k - 1].astype(f32)
-    gfull[my_piece] = gsum.astype(bf16)
-    gkeys = [send(gfull.at[my_piece], gfull.at[my_piece], chip_dev(k)) for k in range(1, CHIPS)]
-    res_keys = [send(rows2(res_ref, up(sx, k)), res_s.at[:, :, cols(sx)], line(k)) for k in (2, 1, 3)]
-    res_s[:, :, cols(sx)] = res_ref[:, pl.ds(pl.multiple_of(sx * pr, pr), pr)]
-    copy_p.wait()
-    for key, k in zip(p_keys, (2, 1, 3)):
-        arrive(key, w.at[2:4, y, z, :, cols(up(sx, -k))])
-    gpa.start()
-    gpb.start()
     ga.finish()
     gb.finish()
+
     wide = N_LAYER * rank
     wa = w[0].reshape(feats, wide)
     wb = w[1].reshape(feats, wide)
@@ -336,6 +317,13 @@
     prod[:, wide:both_x] = dot_nn(xv, wb)
     prod_out[:, 0:both_x] = prod[its_rows, 0:both_x].astype(bf16)
     key_px = send(prod_out.at[:, 0:both_x], prod_in.at[:, 0:both_x], sib)
+    for key, k in zip(gkeys, (2, 1, 3)):
+        arrive(key, gline_in.at[k - 1])
+        gsum = gsum + gline_in[k - 1].astype(f32)
+    gfull[my_piece] = gsum.astype(bf16)
+    gkeys = [send(gfull.at[my_piece], gfull.at[my_piece], chip_dev(k)) for k in range(1, CHIPS)]
+    gpa.second()
+    gpb.second()
     prod[:, both_x:] = dot_nn(yv, wb)
     prod_out[:, both_x:] = prod[its_rows, both_x:].astype(bf16)
     key_py = send(prod_out.at[:, both_x:], prod_in.at[:, both_x:], sib)
@@ -357,8 +345,8 @@
     for k in range(1, CHIPS):
         arrive(gkeys[k - 1], gfull.at[c * CHIPS + chip_back(k)])
     key_gfull = send(gfull.at[my_gram], gfull.at[my_gram], sib)
-    gpa.second_direct()
-    gpb.second_direct()
+    gpa.relay()
+    gpb.relay()
     token_rows = pl.ds(pl.multiple_of(c * tseq + sx * tq, tq), tq)
 
     def line_sum(keys, at):
@@ -444,8 +432,8 @@
             h = hb16.astype(f32) + dot_nt(wq(1, l, q), av[l])
         ht[2 * N_LAYER - 1, fr, :] = (h - yt[fr, :].astype(f32)).astype(bf16)
     key = share(qkeys, q_cols)
-    gpa.finish_direct()
-    gpb.finish_direct()
+    gpa.finish()
+    gpb.finish()
     arrive(key, act.at[its_rows, q_cols])
     qv = [act[:, (N_LAYER + l) * rank : (N_LAYER + l + 1) * rank] for l in range(N_LAYER)]
     gain_t = act[:, 2 * N_LAYER * rank :].astype(f32).T
@@ -593,9 +581,7 @@
     keys = [send(stat2_out, stat2_in.at[k - 1], chip_dev(k)) for k in range(1, CHIPS)]
     for s in both:
         s.done()
-    big_vmem[...] = gx[...].astype(f32).reshape(2, own, rank) * shrink + direc
-    copy_big = pltpu.make_async_copy(big_vmem, big_hbm, local_sem.at[5])
-    copy_big.start()
+    big = gx[...].astype(f32).reshape(2, own, rank) * shrink + direc
     for k in range(1, CHIPS):
         arrive(keys[k - 1], stat2_in.at[k - 1])
         total = total + stat2_in[k - 1]
@@ -605,9 +591,10 @@
     pp = jnp.sum(total[3:4], keepdims=True)
     step = rr / pq * damping
     norm_new = rr - 2.0 * (step * rp) + step * (step * pp)
-    row = lax.broadcasted_iota(jnp.int32, (8, rank), 0)
-    coef_ref[...] = jnp.where(row == 0, step, norm_new / rr)
-    copy_big.wait()
+    new_res = res - step * big
+    newres_ref[...] = new_res
+    newdir_ref[...] = new_res + (norm_new / rr) * direc
+    assert counter.n == N_SEM, counter.n
     for copy in pending:
         copy.wait_send()
 
@@ -633,7 +620,7 @@
         vm((2 * CHIPS, hr, rank), f32), vm((CHIPS, hr, rank), bf16), vm((CHIPS, hr, rank), bf16),
         vm((CHIPS, hr, rank), bf16), vm((CHIPS - 1, hr, rank), bf16), vm((hr, rank), bf16),
         vm((N_LAYER - 1, hr, rank), bf16), vm((2 * CHIPS, hr, rank), bf16),
-        vm((2, pr, wide), f32), vm((2, own, rank), f32),
+        vm((2, pr, wide), f32),
         vm((2 * tseq, 2 * wide + rank), bf16), vm((2 * N_LAYER, feats, 2 * tseq), bf16),
         vm((2, SIDE, SIDE, pr, wide), bf16),
         vm((2, 6, 2, pr, wide), bf16),
@@ -645,19 +632,19 @@
         pltpu.SemaphoreType.DMA((N_SEM,)), pltpu.SemaphoreType.DMA((N_SEM,)), pltpu.SemaphoreType.DMA((8,)),
     ]
     hbm = pl.BlockSpec(memory_space=pl.ANY)
-    big, coef = pl.pallas_call(
+    spec = pl.BlockSpec(memory_space=pltpu.VMEM)
+    out = jax.ShapeDtypeStruct((2, own, rank), f32)
+    new_res, new_dir = pl.pallas_call(
         kernel,
-        out_shape=(jax.ShapeDtypeStruct((2, own, rank), f32), jax.ShapeDtypeStruct((8, rank), f32)),
+        out_shape=(out, out),
         in_specs=[hbm] * 6,
-        out_specs=(hbm, pl.BlockSpec(memory_space=pltpu.VMEM)),
+        out_specs=(spec, spec),
         scratch_shapes=scratch,
         compiler_params=pltpu.CompilerParams(
             collective_id=0, has_side_effects=True, vmem_limit_bytes=58 * 1024 * 1024
         ),
         cost_estimate=pl.CostEstimate(flops=4_000_000_000, bytes_accessed=8_000_000, transcendentals=0),
     )(inputs, targets, down_proj[0], up_proj[0], direction[0], residual[0])
-    new_res = residual[0] - coef[0, 0] * big
-    new_dir = new_res + coef[1, 0] * direction[0]
     return new_res[None], new_dir[None]
 
 

time: 89.2 us -> 88.2 us (0.989)
  other arithmetic: 3.04 us -> 0 us
  local copies, waits for them, and re-layouts: 1.31 us -> 3.34 us
    unnamed x4 -> x2, local copies, waits for them, and re-layouts: 0.01 us -> 3.34 us
    broadcast_in_dim x1 -> x0, other arithmetic: 3.04 us -> none  [step_kernel(): return (new_res[None], new_dir[None])]
    slice x1 -> x0, local copies, waits for them, and re-layouts: 1.3 us -> none  [step_kernel(): new_dir = new_res + coef[1, 0] * direction[0]]
where the time goes in v5:
time: 88.2 us; the launch traced here: 87.9 us
  Pallas kernels  84 us (95%)
  local copies, waits for them, and re-layouts  3.34 us (4%)
    pallas_call x1, Pallas kernels, step_kernel(): pl.pallas_call(kernel, out_shape=(out, out), in_specs=[hbm] * 6, out_spec...  84 us
    unnamed x2, local copies, waits for them, and re-layouts  3.34 us

profile of v5, /device:TPU:1, one launch (start us, length us, event | category | flops | bytes accessed | tf_op | source)
XLA Modules:
  0.0 87.9 jit_solution(15220426345400687134)
XLA Ops:
  0.6 84.0 %shard_map.77 = (f32[2,256,128]{2,1,0:T(8,128)}, f32[2,256,128]{2,1,0:T(8,128)}) custom-call(bf16[128,8192]{1,0:T(8,128)(2,1)} %x_hbm.1, bf16[128,8192]{1,0:T(8,128)(2,1)} %y_hbm.1, bf16[256,128]{1,0:T(8,128)(2,1)} %bitcast.10, bf16[256,128]{1,0:T(8,128)(2,1)} %bitcast.11, f32[2,256,128]{2,1,0:T(8,128)} %bitcast.8, f32[2,256,128]{2,1,0:T(8,128)} %bitcast.9), custom_call_target="tpu_custom_call" | custom-call | flops 4000000000 | bytes 8000000 | tf_op jit(solution)/shard_map/pallas_call | solution.py:637
  84.6 1.7 %copy.10 = f32[1,2,256,128]{3,2,1,0:T(8,128)} copy(f32[1,2,256,128]{3,2,1,0:T(8,128)} %bitcast.7) | data formatting | bytes 524288
  86.3 1.7 %copy.11 = f32[1,2,256,128]{3,2,1,0:T(8,128)} copy(f32[1,2,256,128]{3,2,1,0:T(8,128)} %bitcast.6) | data formatting | bytes 524288

commit v6 on v5

--- a/solution.py
+++ b/solution.py
@@ -49,7 +49,7 @@
         return self.n - 1
 
 
-N_SEM = 154
+N_SEM = 98
 
 
 def kernel(
@@ -118,6 +118,27 @@
         pending.append(copy)
         return k
 
+    def send_all(triples):
+        k = counter.take()
+        for src, dst, dev in triples:
+            pltpu.make_async_remote_copy(
+                src_ref=src, dst_ref=dst, send_sem=send_sem.at[k], recv_sem=recv_sem.at[k],
+                device_id=dev, device_id_type=MESH,
+            ).start()
+        return k
+
+    def arrive_all(k, whole):
+        copy = pltpu.make_async_remote_copy(
+            src_ref=whole, dst_ref=whole, send_sem=send_sem.at[k], recv_sem=recv_sem.at[k],
+            device_id=(sx, f), device_id_type=MESH,
+        )
+        copy.wait_recv()
+        pending.append(copy)
+
+    def flush():
+        while pending:
+            pending.pop(0).wait_send()
+
     def arrive(k, dst):
         pltpu.make_async_remote_copy(
             src_ref=dst, dst_ref=dst, send_sem=send_sem.at[k], recv_sem=recv_sem.at[k],
@@ -188,6 +209,8 @@
                 arrive(self.key[i], self.block(-i))
             self.push("r1", self.pair(0, 0), 0, 1)
             self.push("l1", self.pair(1, 0), 0, -1)
+
+        def second_rest(self):
             self.push("r2", self.pair(1, 0), 0, 1)
             self.push("l2", self.pair(0, 0), 0, -1)
 
@@ -265,12 +288,11 @@
     def chip_dev(k):
         return (sx, fs(up(y, k // SIDE), up(z, k % SIDE), c))
 
-    def chip_back(k):
-        return up(y, -(k // SIDE)) * SIDE + up(z, -(k % SIDE))
-
     ga.second()
     gb.second()
-    gkeys = [send(gramx_out.at[chip(k)], gramx_in.at[k - 1], chip_dev(k)) for k in range(1, CHIPS)]
+    gkey = send_all([(gramx_out.at[chip(k)], gramx_in.at[k - 1], chip_dev(k)) for k in range(1, CHIPS)])
+    ga.second_rest()
+    gb.second_rest()
     xq = xin[pl.ds(pl.multiple_of(sx * tq, tq), tq), :].astype(f32)
     norm = jnp.sum(xq * xq, axis=1, keepdims=True)
     load_r.wait()
@@ -288,6 +310,11 @@
     arrive(key_ys, yg.at[its_rows])
     xt[...] = xg[...].astype(f32).T.astype(bf16)
     yt[...] = yg[...].astype(f32).T.astype(bf16)
+    my_piece = c * CHIPS + y * SIDE + z
+    arrive_all(gkey, gramx_in)
+    gsum = gram[my_piece] + jnp.sum(gramx_in[...].astype(f32), axis=0)
+    gline_out[...] = gsum.astype(bf16)
+    gkey = send_all([(gline_out, gline_in.at[k - 1], line(k)) for k in (2, 1, 3)])
     ga.relay()
     gb.relay()
     copy_p.wait()
@@ -295,15 +322,11 @@
         arrive(key, w.at[2:4, y, z, :, cols(up(sx, -k))])
     gpa.start()
     gpb.start()
+    arrive_all(gkey, gline_in)
+    gfull[my_piece] = (gsum + jnp.sum(gline_in[...].astype(f32), axis=0)).astype(bf16)
+    gkey = send_all([(gfull.at[my_piece], gfull.at[my_piece], chip_dev(k)) for k in range(1, CHIPS)])
     res_keys = [send(rows2(res_ref, up(sx, k)), res_s.at[:, :, cols(sx)], line(k)) for k in (2, 1, 3)]
     res_s[:, :, cols(sx)] = res_ref[:, pl.ds(pl.multiple_of(sx * pr, pr), pr)]
-    my_piece = c * CHIPS + y * SIDE + z
-    gsum = gram[my_piece]
-    for k in range(1, CHIPS):
-        arrive(gkeys[k - 1], gramx_in.at[k - 1])
-        gsum = gsum + gramx_in[k - 1].astype(f32)
-    gline_out[...] = gsum.astype(bf16)
-    gkeys = [send(gline_out, gline_in.at[k - 1], line(k)) for k in (2, 1, 3)]
     ga.finish()
     gb.finish()
 
@@ -317,13 +340,10 @@
     prod[:, wide:both_x] = dot_nn(xv, wb)
     prod_out[:, 0:both_x] = prod[its_rows, 0:both_x].astype(bf16)
     key_px = send(prod_out.at[:, 0:both_x], prod_in.at[:, 0:both_x], sib)
-    for key, k in zip(gkeys, (2, 1, 3)):
-        arrive(key, gline_in.at[k - 1])
-        gsum = gsum + gline_in[k - 1].astype(f32)
-    gfull[my_piece] = gsum.astype(bf16)
-    gkeys = [send(gfull.at[my_piece], gfull.at[my_piece], chip_dev(k)) for k in range(1, CHIPS)]
     gpa.second()
     gpb.second()
+    gpa.second_rest()
+    gpb.second_rest()
     prod[:, both_x:] = dot_nn(yv, wb)
     prod_out[:, both_x:] = prod[its_rows, both_x:].astype(bf16)
     key_py = send(prod_out.at[:, both_x:], prod_in.at[:, both_x:], sib)
@@ -342,8 +362,7 @@
     in_x, in_y = slice(0, both_x), slice(both_x, 3 * wide)
     pxkeys = pair_sum(key_px, in_x)
     pykeys = pair_sum(key_py, in_y)
-    for k in range(1, CHIPS):
-        arrive(gkeys[k - 1], gfull.at[c * CHIPS + chip_back(k)])
+    arrive_all(gkey, gfull.at[0 : CHIPS - 1])
     key_gfull = send(gfull.at[my_gram], gfull.at[my_gram], sib)
     gpa.relay()
     gpb.relay()
@@ -461,13 +480,10 @@
         return jnp.concatenate([fold(v) for v in values] + [jnp.zeros((8 - len(values), rank), f32)], axis=0)
 
     dv_out[...] = stack([d0, d1])
-    keys = []
-    for k in range(1, 8):
-        keys.append(send(dv_out, dv_in.at[k - 1], (up(sx, k // 2), fs(y, z, lax.rem(c + k, 2)))))
-    dv = dv_out[...]
-    for k in range(1, 8):
-        arrive(keys[k - 1], dv_in.at[k - 1])
-        dv = dv + dv_in[k - 1]
+    eight = [(up(sx, k // 2), fs(y, z, lax.rem(c + k, 2))) for k in range(1, 8)]
+    key = send_all([(dv_out, dv_in.at[k], dev) for k, dev in enumerate(eight)])
+    arrive_all(key, dv_in)
+    dv = dv_out[...] + jnp.sum(dv_in[...], axis=0)
     s0 = jnp.sum(dv[0:1], keepdims=True) / (tseq * width)
     s1 = jnp.sum(dv[1:2], keepdims=True) / (tseq * width)
     token = lax.broadcasted_iota(jnp.int32, (2 * tseq, 1), 0)
@@ -547,6 +563,7 @@
     both[0].start()
     gradient(1, N_LAYER, ad)
     both[1].start()
+    flush()
     for s in both:
         s.middle()
     for s in both:
@@ -570,21 +587,18 @@
     stat_out[...] = home + jnp.concatenate(
         [jnp.zeros((1, rank), f32), pg, rg, 2.0 * pg + gg, jnp.zeros((4, rank), f32)], axis=0
     )
-    keys = []
-    for k in range(1, 8):
-        keys.append(send(stat_out, stat_in.at[k - 1], (up(sx, k // 2), fs(y, z, lax.rem(c + k, 2)))))
-    total = stat_out[...]
-    for k in range(1, 8):
-        arrive(keys[k - 1], stat_in.at[k - 1])
-        total = total + stat_in[k - 1]
+    key = send_all([(stat_out, stat_in.at[k], dev) for k, dev in enumerate(eight)])
+    flush()
+    arrive_all(key, stat_in)
+    total = stat_out[...] + jnp.sum(stat_in[...], axis=0)
     stat2_out[...] = total
-    keys = [send(stat2_out, stat2_in.at[k - 1], chip_dev(k)) for k in range(1, CHIPS)]
+    key = send_all([(stat2_out, stat2_in.at[k - 1], chip_dev(k)) for k in range(1, CHIPS)])
     for s in both:
         s.done()
     big = gx[...].astype(f32).reshape(2, own, rank) * shrink + direc
-    for k in range(1, CHIPS):
-        arrive(keys[k - 1], stat2_in.at[k - 1])
-        total = total + stat2_in[k - 1]
+    flush()
+    arrive_all(key, stat2_in)
+    total = total + jnp.sum(stat2_in[...], axis=0)
     rr = jnp.sum(total[0:1], keepdims=True)
     pq = jnp.sum(total[1:2], keepdims=True) * damping
     rp = jnp.sum(total[2:3], keepdims=True)
@@ -594,9 +608,8 @@
     new_res = res - step * big
     newres_ref[...] = new_res
     newdir_ref[...] = new_res + (norm_new / rr) * direc
-    assert counter.n == N_SEM, counter.n
-    for copy in pending:
-        copy.wait_send()
+    assert counter.n == N_SEM
+    flush()
 
 
 def step_kernel(inputs, targets, down_proj, up_proj, direction, residual):

time: 88.2 us -> 86.5 us (0.981)
  Pallas kernels: 84 us -> 82.3 us
    pallas_call x1, Pallas kernels: 84 us -> 82.3 us  [step_kernel(): pl.pallas_call(kernel, out_shape=(out, out), in_specs=[hbm] * 6, out_spec...]
where the time goes in v6:
time: 86.5 us; the launch traced here: 86.3 us
  Pallas kernels  82.3 us (95%)
  local copies, waits for them, and re-layouts  3.34 us (4%)
    pallas_call x1, Pallas kernels, step_kernel(): pl.pallas_call(kernel, out_shape=(out, out), in_specs=[hbm] * 6, out_spec...  82.3 us
    unnamed x2, local copies, waits for them, and re-layouts  3.34 us

profile of v6, /device:TPU:1, one launch (start us, length us, event | category | flops | bytes accessed | tf_op | source)
XLA Modules:
  0.0 86.3 jit_solution(9014222718849795765)
XLA Ops:
  0.6 82.3 %shard_map.77 = (f32[2,256,128]{2,1,0:T(8,128)}, f32[2,256,128]{2,1,0:T(8,128)}) custom-call(bf16[128,8192]{1,0:T(8,128)(2,1)} %x_hbm.1, bf16[128,8192]{1,0:T(8,128)(2,1)} %y_hbm.1, bf16[256,128]{1,0:T(8,128)(2,1)} %bitcast.10, bf16[256,128]{1,0:T(8,128)(2,1)} %bitcast.11, f32[2,256,128]{2,1,0:T(8,128)} %bitcast.8, f32[2,256,128]{2,1,0:T(8,128)} %bitcast.9), custom_call_target="tpu_custom_call" | custom-call | flops 4000000000 | bytes 8000000 | tf_op jit(solution)/shard_map/pallas_call | solution.py:650
  82.9 1.7 %copy.10 = f32[1,2,256,128]{3,2,1,0:T(8,128)} copy(f32[1,2,256,128]{3,2,1,0:T(8,128)} %bitcast.7) | data formatting | bytes 524288
  84.6 1.7 %copy.11 = f32[1,2,256,128]{3,2,1,0:T(8,128)} copy(f32[1,2,256,128]{3,2,1,0:T(8,128)} %bitcast.6) | data formatting | bytes 524288

commit v7 on v6

--- a/solution.py
+++ b/solution.py
@@ -646,7 +646,8 @@
     ]
     hbm = pl.BlockSpec(memory_space=pl.ANY)
     spec = pl.BlockSpec(memory_space=pltpu.VMEM)
-    out = jax.ShapeDtypeStruct((2, own, rank), f32)
+    operands = (inputs, targets, down_proj[0], up_proj[0], direction[0], residual[0])
+    out = pltpu.VMEM((2, own, rank), f32)
     new_res, new_dir = pl.pallas_call(
         kernel,
         out_shape=(out, out),
@@ -654,10 +655,10 @@
         out_specs=(spec, spec),
         scratch_shapes=scratch,
         compiler_params=pltpu.CompilerParams(
-            collective_id=0, has_side_effects=True, vmem_limit_bytes=58 * 1024 * 1024
+            collective_id=0, has_side_effects=True, vmem_limit_bytes=50 * 1024 * 1024
         ),
         cost_estimate=pl.CostEstimate(flops=4_000_000_000, bytes_accessed=8_000_000, transcendentals=0),
-    )(inputs, targets, down_proj[0], up_proj[0], direction[0], residual[0])
+    )(*(pltpu.with_memory_space_constraint(v, pltpu.HBM) for v in operands))
     return new_res[None], new_dir[None]
 
 

time: 86.5 us -> 83.7 us (0.968)
  local copies, waits for them, and re-layouts: 3.34 us -> 1.41 us
    unnamed x2, local copies, waits for them, and re-layouts: 3.34 us -> 1.41 us
where the time goes in v7:
time: 83.7 us; the launch traced here: 83.6 us
  Pallas kernels  81.5 us (97%)
  local copies, waits for them, and re-layouts  1.41 us (2%)
    pallas_call x1, Pallas kernels, step_kernel(): pl.pallas_call(kernel, out_shape=(out, out), in_specs=[hbm] * 6, out_spec...  81.5 us

profile of v7, /device:TPU:1, one launch (start us, length us, event | category | flops | bytes accessed | tf_op | source)
XLA Modules:
  0.0 83.6 jit_solution(12324346643742426840)
XLA Ops:
  0.6 81.5 %shard_map.77 = (f32[2,256,128]{2,1,0:T(8,128)S(1)}, f32[2,256,128]{2,1,0:T(8,128)S(1)}) custom-call(bf16[128,8192]{1,0:T(8,128)(2,1)} %x_hbm.1, bf16[128,8192]{1,0:T(8,128)(2,1)} %y_hbm.1, bf16[256,128]{1,0:T(8,128)(2,1)} %bitcast.10, bf16[256,128]{1,0:T(8,128)(2,1)} %bitcast.11, f32[2,256,128]{2,1,0:T(8,128)} %bitcast.8, f32[2,256,128]{2,1,0:T(8,128)} %bitcast.9), custom_call_target="tpu_custom_call" | custom-call | flops 4000000000 | bytes 8000000 | tf_op jit(solution)/shard_map/pallas_call | solution.py:651
  82.1 0.7 copy.10
  82.8 0.7 copy.11

commit v8 on v7

--- a/solution.py
+++ b/solution.py
@@ -456,17 +456,22 @@
     arrive(key, act.at[its_rows, q_cols])
     qv = [act[:, (N_LAYER + l) * rank : (N_LAYER + l + 1) * rank] for l in range(N_LAYER)]
     gain_t = act[:, 2 * N_LAYER * rank :].astype(f32).T
-    d0 = jnp.zeros((quad, rank), f32)
-    d1 = jnp.zeros((quad, rank), f32)
+    first = lax.broadcasted_iota(jnp.int32, (2 * tseq, rank), 0) < tseq
+
+    def apart(v):
+        none = jnp.zeros_like(v)
+        return jnp.concatenate([jnp.where(first, v, none), jnp.where(first, none, v)], axis=1)
+
+    apart_q, apart_a = [apart(v) for v in qv], [apart(v) for v in av]
+    both_d = jnp.zeros((quad, 2 * rank), f32)
     for q in range(SIDE):
         fr = slice(q * quad, (q + 1) * quad)
         cot = ht[2 * N_LAYER - 1, fr, :]
         for l in range(N_LAYER - 1, -1, -1):
             hl = ht[l, fr, :]
-            for arr, left, right in ((2, hl, qv[l]), (3, cot, av[l])):
+            for arr, left, right in ((2, hl, apart_q[l]), (3, cot, apart_a[l])):
                 pw = wq(arr, l, q).astype(f32)
-                d0 = d0 + dot_nn(left[:, :tseq], right[:tseq]) * pw
-                d1 = d1 + dot_nn(left[:, tseq:], right[tseq:]) * pw
+                both_d = both_d + dot_nn(left, right) * jnp.concatenate([pw, pw], axis=1)
             if l > 0:
                 cot = (
                     cot.astype(f32) + dot_nt(wq(0, l, q), qv[l]) - gain_t[l : l + 1, :] * hl.astype(f32)
@@ -479,7 +484,7 @@
     def stack(values):
         return jnp.concatenate([fold(v) for v in values] + [jnp.zeros((8 - len(values), rank), f32)], axis=0)
 
-    dv_out[...] = stack([d0, d1])
+    dv_out[...] = stack([both_d[:, :rank], both_d[:, rank:]])
     eight = [(up(sx, k // 2), fs(y, z, lax.rem(c + k, 2))) for k in range(1, 8)]
     key = send_all([(dv_out, dv_in.at[k], dev) for k, dev in enumerate(eight)])
     arrive_all(key, dv_in)
@@ -491,11 +496,12 @@
     qd = [(qv[l].astype(f32) * scale).astype(bf16) for l in range(N_LAYER)]
     ad = [(av[l].astype(f32) * scale).astype(bf16) for l in range(N_LAYER)]
 
-    def gradient(arr, base, right):
+    def gradient(arr, q):
+        base, right = ((0, qd), (N_LAYER, ad))[arr]
+        at = pl.ds(pl.multiple_of(q * quad, quad), quad)
         for l in range(N_LAYER):
-            for q in range(SIDE):
-                value = dot_nn(ht[base + l, q * quad : (q + 1) * quad, :], right[l])
-                g[arr, q, :, :, l * rank : (l + 1) * rank] = value.astype(bf16).reshape(SIDE, pr, rank)
+            value = dot_nn(ht[base + l, at, :], right[l])
+            g[arr, q, :, :, l * rank : (l + 1) * rank] = value.astype(bf16).reshape(SIDE, pr, rank)
 
     class Scatter:
         def __init__(self, arr, last):
@@ -518,11 +524,8 @@
             arrive(self.key[n], pair_in.at[self.arr, n])
             return pair_in[self.arr, n].astype(f32)
 
-        def start(self):
-            self.push(0, 0, 2, 1)
-            self.push(1, 1, 2, -1)
-            self.push(2, 1, 1, 1)
-            self.push(3, 0, -1, -1)
+        def start(self, n):
+            self.push(n, *((0, 2, 1), (1, 2, -1), (1, 1, 1), (0, -1, -1))[n])
 
         def middle(self):
             at = self.pair(0, 1)
@@ -559,10 +562,21 @@
                 arrive(self.back[k - 1], gx.at[self.arr, up(sx, -k)])
 
     both = (Scatter(0, "y"), Scatter(1, "z"))
-    gradient(0, 0, qd)
-    both[0].start()
-    gradient(1, N_LAYER, ad)
-    both[1].start()
+    gradient(1, up(y, 2))
+    both[1].start(0)
+    both[1].start(1)
+    for q in range(2):
+        gradient(0, q)
+    both[0].start(0)
+    for q in range(2, SIDE):
+        gradient(0, q)
+    for n in range(1, SIDE):
+        both[0].start(n)
+    gradient(1, up(y, 1))
+    both[1].start(2)
+    gradient(1, up(y, -1))
+    both[1].start(3)
+    gradient(1, y)
     flush()
     for s in both:
         s.middle()

time: 83.7 us -> 82.9 us (level)
  no operation moved by 1% of the time
where the time goes in v8:
time: 82.9 us; the launch traced here: 82.7 us
  Pallas kernels  80.7 us (97%)
  local copies, waits for them, and re-layouts  1.41 us (2%)
    pallas_call x1, Pallas kernels, step_kernel(): pl.pallas_call(kernel, out_shape=(out, out), in_specs=[hbm] * 6, out_spec...  80.7 us

profile of v8, /device:TPU:1, one launch (start us, length us, event | category | flops | bytes accessed | tf_op | source)
XLA Modules:
  0.0 82.7 jit_solution(12817246311877296050)
XLA Ops:
  0.6 80.7 %shard_map.77 = (f32[2,256,128]{2,1,0:T(8,128)S(1)}, f32[2,256,128]{2,1,0:T(8,128)S(1)}) custom-call(bf16[128,8192]{1,0:T(8,128)(2,1)} %x_hbm.1, bf16[128,8192]{1,0:T(8,128)(2,1)} %y_hbm.1, bf16[256,128]{1,0:T(8,128)(2,1)} %bitcast.10, bf16[256,128]{1,0:T(8,128)(2,1)} %bitcast.11, f32[2,256,128]{2,1,0:T(8,128)} %bitcast.8, f32[2,256,128]{2,1,0:T(8,128)} %bitcast.9), custom_call_target="tpu_custom_call" | custom-call | flops 4000000000 | bytes 8000000 | tf_op jit(solution)/shard_map/pallas_call | solution.py:665
  81.3 0.7 copy.10
  82.0 0.7 copy.11

commit v9 on v8

--- a/solution.py
+++ b/solution.py
@@ -550,7 +550,9 @@
                 arrive(self.key[("s", i)], block_in.at[self.arr, i % SIDE - 1])
                 value = value + block_in[self.arr, i % SIDE - 1].astype(f32)
             self.value = value
-            fin[self.arr, SIDE] = value.astype(bf16)
+
+        def home(self):
+            fin[self.arr, SIDE] = self.value.astype(bf16)
             self.back = []
             for k in range(1, N_LAYER):
                 to = up(sx, k)
@@ -602,7 +604,8 @@
         [jnp.zeros((1, rank), f32), pg, rg, 2.0 * pg + gg, jnp.zeros((4, rank), f32)], axis=0
     )
     key = send_all([(stat_out, stat_in.at[k], dev) for k, dev in enumerate(eight)])
-    flush()
+    for s in both:
+        s.home()
     arrive_all(key, stat_in)
     total = stat_out[...] + jnp.sum(stat_in[...], axis=0)
     stat2_out[...] = total

time: 82.9 us -> 82.2 us (level)
  no operation moved by 1% of the time
where the time goes in v9:
time: 82.2 us; the launch traced here: 82 us
  Pallas kernels  80 us (97%)
  local copies, waits for them, and re-layouts  1.41 us (2%)
    pallas_call x1, Pallas kernels, step_kernel(): pl.pallas_call(kernel, out_shape=(out, out), in_specs=[hbm] * 6, out_spec...  80 us

profile of v9, /device:TPU:1, one launch (start us, length us, event | category | flops | bytes accessed | tf_op | source)
XLA Modules:
  0.0 82.0 jit_solution(5916587006656450303)
XLA Ops:
  0.6 80.0 %shard_map.77 = (f32[2,256,128]{2,1,0:T(8,128)S(1)}, f32[2,256,128]{2,1,0:T(8,128)S(1)}) custom-call(bf16[128,8192]{1,0:T(8,128)(2,1)} %x_hbm.1, bf16[128,8192]{1,0:T(8,128)(2,1)} %y_hbm.1, bf16[256,128]{1,0:T(8,128)(2,1)} %bitcast.10, bf16[256,128]{1,0:T(8,128)(2,1)} %bitcast.11, f32[2,256,128]{2,1,0:T(8,128)} %bitcast.8, f32[2,256,128]{2,1,0:T(8,128)} %bitcast.9), custom_call_target="tpu_custom_call" | custom-call | flops 4000000000 | bytes 8000000 | tf_op jit(solution)/shard_map/pallas_call | solution.py:668
  80.6 0.7 copy.10
  81.3 0.7 copy.11
